TPU v7x, 256 devices: a whole 4x4x8 slice. The times are simulated.
256 devices in a mesh: wide: 32 (over x, z), narrow: 8 (over y, core).
Axes of the slice: x: 4, y: 4, z: 8, core: 2. Of those that a mesh axis runs over, the one named last changes fastest.
Arguments:
- records: bfloat16 [32, 512, 49152], P(None, 'narrow', 'wide'), may hold values from -6 to 6
- taps: float32 [201], replicated, may hold values from -0.4375 to 0.4375
- pair_sources: int32 [32, 4], replicated, may hold values from 0 to 31, as said below
- pair_counts: int32 [32], P('wide'), may hold values from 1 to 4, as said below
Outputs:
- correlations: bfloat16 [32, 4, 512, 32, 256], P('wide', None, 'narrow')
Inputs may be any that keep to these rules, and one draw needn't show every extreme that they name: `pair_sources`: each row lists 4 different blocks; only the first pair_counts[r] of row r are paired with r. `pair_counts`: some block has 4 pairs in every draw.
All inputs are finite; a program needn't handle non-finite values.
Results may differ from a plain program's by a relative error of at most 0.0096.
Values may be sent and summed in bfloat16 or wider, within the bound.
A program may use at most 128 MiB of HBM per device.

v0:
```python
import math

import jax
import jax.numpy as jnp
from jax import lax
from jax.sharding import PartitionSpec as P

BLOCK_CHANNELS = 512
VIRTUAL_SOURCES = 32
TAPS = 201
WLEN = 512
FREQUENCY_BINS = 128
F_LO = 4
LAG_COUNT = 256
MAX_PAIRED_SRC = 4


def shifted(shard, axis, by):
    count = lax.axis_size(axis)
    pairs = [(i, i + by) for i in range(count) if 0 <= i + by < count]
    return lax.ppermute(shard, axis, pairs)


def taps_matrix(taps):
    kernel = taps.astype(jnp.bfloat16)
    span = WLEN + TAPS - 1
    padded = jnp.concatenate([kernel[::-1], jnp.zeros((WLEN,), kernel.dtype)])
    tiled = jnp.tile(padded, WLEN)[: WLEN * span].reshape(WLEN, span)
    return tiled.T


def dft_table():
    times = jnp.arange(WLEN, dtype=jnp.int32)[:, None]
    bins = (F_LO + jnp.arange(FREQUENCY_BINS, dtype=jnp.int32))[None, :]
    phase = jnp.mod(times * bins, WLEN)
    angle = phase.astype(jnp.float32) * (2.0 * math.pi / WLEN)
    scale = 1.0 / math.sqrt(WLEN)
    return jnp.concatenate([jnp.cos(angle) * scale, -jnp.sin(angle) * scale], 1).astype(
        jnp.bfloat16
    )


def lag_table():
    bins = (F_LO + jnp.arange(FREQUENCY_BINS, dtype=jnp.int32))[:, None]
    lags = (jnp.arange(LAG_COUNT, dtype=jnp.int32) - LAG_COUNT // 2)[None, :]
    phase = jnp.mod(bins * lags, WLEN)
    angle = phase.astype(jnp.float32) * (2.0 * math.pi / WLEN)
    scale = 1.0 / math.sqrt(FREQUENCY_BINS)
    return jnp.concatenate([jnp.cos(angle) * scale, -jnp.sin(angle) * scale], 0).astype(
        jnp.bfloat16
    )


def cross_spectra(recv, source_indices, count):
    rec_re = recv[:, :, 0]
    rec_im = recv[:, :, 1]
    src_re = source_indices[:, :, :, 0]
    src_im = source_indices[:, :, :, 1]
    form = "iwf,kjwf->kijf"
    real = jnp.einsum(form, rec_re, src_re, preferred_element_type=jnp.float32) + jnp.einsum(
        form, rec_im, src_im, preferred_element_type=jnp.float32
    )
    imag = jnp.einsum(form, rec_im, src_re, preferred_element_type=jnp.float32) - jnp.einsum(
        form, rec_re, src_im, preferred_element_type=jnp.float32
    )
    scale = 1.0 / math.sqrt(recv.shape[1])
    live = (jnp.arange(MAX_PAIRED_SRC, dtype=jnp.int32) < count).astype(jnp.float32)[
        :, None, None, None
    ]
    return jnp.stack([real * scale * live, imag * scale * live], 3).astype(jnp.bfloat16)


def on_device(records, taps, pair_sources, pair_counts):
    channel_blocks, subset_channels, time_dev = records.shape
    windows_per_shard = time_dev // WLEN
    main = records.reshape(channel_blocks * subset_channels, windows_per_shard, WLEN)
    tails = main[:, :, WLEN - (TAPS - 1) :]
    history = shifted(tails[:, windows_per_shard - 1], "wide", 1)
    previous = jnp.concatenate([history[:, None], tails[:, : windows_per_shard - 1]], 1)
    windows = jnp.concatenate([previous, main], 2)
    whitened = jnp.dot(windows, taps_matrix(taps), preferred_element_type=jnp.float32).astype(
        jnp.bfloat16
    )
    block_spectrum = jnp.dot(whitened, dft_table(), preferred_element_type=jnp.float32).astype(
        jnp.bfloat16
    )
    block_spectrum = block_spectrum.reshape(
        channel_blocks, subset_channels, windows_per_shard, 2, FREQUENCY_BINS
    )
    virtual_channels = block_spectrum[:, :: BLOCK_CHANNELS // VIRTUAL_SOURCES]
    source_slots = pair_sources.reshape(-1)
    count = pair_counts[0]
    finished_pairs = lax.all_gather(virtual_channels, "narrow", axis=1, tiled=True)
    picked_sources = jnp.take(finished_pairs, source_slots, axis=0).reshape(
        channel_blocks, MAX_PAIRED_SRC * VIRTUAL_SOURCES, windows_per_shard, 2, FREQUENCY_BINS
    )
    recv = lax.all_to_all(block_spectrum, "wide", split_axis=0, concat_axis=2, tiled=True)
    source_indices = lax.all_to_all(picked_sources, "wide", split_axis=0, concat_axis=2, tiled=True)
    source_blocks = source_indices[0].reshape(
        MAX_PAIRED_SRC, VIRTUAL_SOURCES, source_indices.shape[2], 2, source_indices.shape[4]
    )
    cross = cross_spectra(recv[0], source_blocks, count)
    lag_domain = jnp.dot(
        cross.reshape(-1, 2 * FREQUENCY_BINS), lag_table(), preferred_element_type=jnp.float32
    )
    return lag_domain.astype(jnp.bfloat16).reshape(
        1, MAX_PAIRED_SRC, subset_channels, VIRTUAL_SOURCES, LAG_COUNT
    )


def solution(mesh):
    return jax.shard_map(
        on_device,
        mesh=mesh,
        in_specs=(P(None, "narrow", "wide"), P(), P(), P("wide")),
        out_specs=P("wide", None, "narrow", None, None),
        check_vma=False,
    )
```

profile of v0, /device:TPU:1, one launch (start us, length us, event | category | flops | bytes accessed | tf_op | source)
XLA Modules:
  0.0 385.6 jit_solution(240673002298415184)
XLA Ops:
  6.5 18.6 %reshape.77 = bf16[2048,3,512]{2,1,0:T(4,128)(2,1)} reshape(bf16[32,64,1536]{2,1,0:T(8,128)(2,1)} %param.4) | data formatting | bytes 12582912 | tf_op jit(solution)/shard_map/reshape | solution.py:76
  25.2 5.5 %slice.37 = bf16[2048,1,200]{2,1,0:T(2,128)(2,1)S(1)} slice(bf16[2048,3,512]{2,1,0:T(4,128)(2,1)} %reshape.77), slice={[0:2048], [2:3], [312:512]} | slice | bytes 1638400 | tf_op jit(solution)/shard_map/slice | solution.py:78
  34.0 5.4 %collective-permute-start = (bf16[2048,200]{0,1:T(8,128)(2,1)}, bf16[2048,200]{0,1:T(8,128)(2,1)}, u32[]{:S(2)}, u32[]{:S(2)}) collective-permute-start(bf16[2048,200]{0,1:T(8,128)(2,1)} %bitcast), channel_id=1, source_target_pairs={{0,8},{8,16},{16,24},{24,32},{32,40},{40,48},{48,56},{56,64},{64,7... | collective-permute-start | bytes 2457608 | tf_op jit(solution)/shard_map/ppermute | solution.py:21
  39.5 13.1 %copy.36 = bf16[2048,3,512]{0,2,1:T(8,128)(2,1)} copy(bf16[2048,3,512]{2,1,0:T(4,128)(2,1)} %reshape.77) | data formatting | bytes 12582912 | tf_op jit(solution)/shard_map/reshape | solution.py:76
  58.8 10.7 %fusion.20 = bf16[2048,3,256]{2,0,1:T(8,128)(2,1)} fusion(bf16[2048,3,512]{0,2,1:T(8,128)(2,1)} %copy.36, bf16[2048,2,200]{0,2,1:T(8,128)(2,1)S(1)} %slice.38, bf16[2048,1,200]{0,2,1:T(8,128)(2,1)} %bitcast.1, bf16[512,712]{1,0:T(8,128)(2,1)S(1)} %reshape.78, bf16[512,128]{1,0:T(8,128)(2,1)S(1)} %get-tuple-element.12, ...), kind=kOutput, calls=%fused_computation.26 | convolution fusion | flops 6121619456 | bytes 12886016 | tf_op jit(solution)/shard_map/dot_general | solution.py:84
  75.8 10.0 %all-to-all-start.1 = ((bf16[32,64,3,2,128]{4,1,3,2,0:T(8,128)(2,1)}), bf16[32,64,3,2,128]{4,1,3,2,0:T(8,128)(2,1)}, u32[]{:S(2)}, u32[]{:S(2)}) async-start(bf16[32,64,3,2,128]{4,1,3,2,0:T(8,128)(2,1)} %copy.45), calls=%async_computation.1 | async-start | bytes 6291456 | tf_op jit(solution)/shard_map/all_to_all | solution.py:97
  87.5 30.8 %all-gather.2.cloned.1.call-done = bf16[32,32,3,2,128]{4,0,3,2,1:T(8,128)(2,1)} async-done(((bf16[32,4,3,2,128]{4,0,3,2,1:T(8,128)(2,1)}), bf16[32,32,3,2,128]{4,0,3,2,1:T(8,128)(2,1)}) %all-gather.2.cloned.1.call-update) | async-done | bytes 1572880 | tf_op jit(solution)/shard_map/all_gather | solution.py:93
  120.7 4.0 %gather_fusion = bf16[128,32,3,2,128]{4,1,3,2,0:T(8,128)(2,1)} fusion(bf16[32,32,3,2,128]{4,1,3,2,0:T(8,128)(2,1)S(1)} %copy.41, s32[1024]{0:T(1024)S(1)} %pad_clamp_fusion), kind=kCustom, calls=%fused_computation | custom fusion | bytes 12583424 | tf_op jit(solution)/shard_map/jit(_take)/gather | solution.py:94
  124.7 4.0 %copy.42 = bf16[128,32,3,2,128]{4,1,0,3,2:T(8,128)(2,1)S(1)} copy(bf16[128,32,3,2,128]{4,1,3,2,0:T(8,128)(2,1)} %gather_fusion) | data formatting | bytes 12582912 | tf_op jit(solution)/shard_map/jit(_take)/gather | solution.py:94
  129.9 4.0 %copy.43 = bf16[32,128,3,2,128]{4,1,3,2,0:T(8,128)(2,1)} copy(bf16[32,128,3,2,128]{4,1,0,3,2:T(8,128)(2,1)S(1)} %bitcast_select_fusion) | data formatting | bytes 12582912 | tf_op jit(solution)/shard_map/jit(_take)/select_n | solution.py:94
  133.9 23.3 %all-to-all-done.1 = bf16[32,64,3,2,128]{4,1,3,2,0:T(8,128)(2,1)} async-done(((bf16[32,64,3,2,128]{4,1,3,2,0:T(8,128)(2,1)}), bf16[32,64,3,2,128]{4,1,3,2,0:T(8,128)(2,1)}, u32[]{:S(2)}, u32[]{:S(2)}) %all-to-all-start.1) | async-done | bytes 3145760 | tf_op jit(solution)/shard_map/all_to_all | solution.py:97
  157.2 7.6 %all-to-all-start = ((bf16[32,128,3,2,128]{4,1,3,2,0:T(8,128)(2,1)}), bf16[32,128,3,2,128]{4,1,3,2,0:T(8,128)(2,1)}, u32[]{:S(2)}, u32[]{:S(2)}) async-start(bf16[32,128,3,2,128]{4,1,3,2,0:T(8,128)(2,1)} %copy.43), calls=%async_computation | async-start | bytes 12582912 | tf_op jit(solution)/shard_map/all_to_all | solution.py:98
  166.0 4.3 %fusion.56 = (bf16[64,96,1,128]{3,0,2,1:T(8,128)(2,1)}, bf16[64,96,1,128]{3,0,2,1:T(8,128)(2,1)}) fusion(bf16[64,96,2,128]{3,0,2,1:T(8,128)(2,1)} %bitcast.12), kind=kLoop, calls=%fused_computation.70 | loop fusion | bytes 6291456 | tf_op jit(solution)/shard_map/slice | solution.py:56
  174.0 4.8 %copy.56 = bf16[64,96,1,128]{1,0,3,2:T(8,128)(2,1)} copy(bf16[64,96,1,128]{3,0,2,1:T(8,128)(2,1)} %get-tuple-element.8) | data formatting | bytes 3145728
  178.7 125.2 %all-to-all-done = bf16[32,128,3,2,128]{4,1,3,2,0:T(8,128)(2,1)} async-done(((bf16[32,128,3,2,128]{4,1,3,2,0:T(8,128)(2,1)}), bf16[32,128,3,2,128]{4,1,3,2,0:T(8,128)(2,1)}, u32[]{:S(2)}, u32[]{:S(2)}) %all-to-all-start) | async-done | bytes 6291488 | tf_op jit(solution)/shard_map/all_to_all | solution.py:98
  304.0 8.1 %fusion.55 = (bf16[4,32,96,1,128]{4,1,0,3,2:T(8,128)(2,1)}, bf16[4,32,96,1,128]{4,1,0,3,2:T(8,128)(2,1)}) fusion(bf16[4,32,96,2,128]{4,1,0,3,2:T(8,128)(2,1)} %bitcast.8), kind=kLoop, calls=%fused_computation.69 | loop fusion | bytes 12582912 | tf_op jit(solution)/shard_map/slice | solution.py:57
  312.1 8.5 %copy.57 = bf16[4,32,96,1,128]{2,1,0,4,3:T(8,128)(2,1)} copy(bf16[4,32,96,1,128]{4,1,0,3,2:T(8,128)(2,1)} %get-tuple-element.6) | data formatting | bytes 6291456
  320.6 8.6 %copy.55 = bf16[4,32,96,1,128]{2,1,0,4,3:T(8,128)(2,1)} copy(bf16[4,32,96,1,128]{4,1,0,3,2:T(8,128)(2,1)} %get-tuple-element.5) | data formatting | bytes 6291456
  329.2 6.8 %fusion.14 = f32[128,4,32,64]{3,2,1,0:T(8,128)} fusion(bf16[4,32,96,1,128]{2,1,0,4,3:T(8,128)(2,1)} %copy.57, bf16[64,96,1,128]{1,0,3,2:T(8,128)(2,1)S(1)} %copy.58), kind=kOutput, calls=%fused_computation.20 | convolution fusion | flops 201326592 | bytes 8912896 | tf_op jit(solution)/shard_map/iwf,kjwf->kijf/dot_general | solution.py:60
  338.2 7.3 %fusion.8 = bf16[4,64,32,1,128]{1,2,0,4,3:T(8,128)(2,1)} fusion(f32[128,4,32,64]{3,2,1,0:T(8,128)} %fusion.14, f32[4]{0:T(128)S(1)} %compare_select_fusion.2, bf16[4,32,96,1,128]{2,1,0,4,3:T(8,128)(2,1)S(1)} %copy-done.1, bf16[64,96,1,128]{1,0,3,2:T(8,128)(2,1)} %copy.56), kind=kOutput, calls=%fused_computation.14 | convolution fusion | flops 204472320 | bytes 11010064 | tf_op jit(solution)/shard_map/iwf,kjwf->kijf/dot_general | solution.py:60
  345.5 4.9 %fusion.9 = bf16[4,64,32,1,128]{1,2,0,4,3:T(8,128)(2,1)} fusion(f32[128,4,32,64]{3,2,1,0:T(8,128)S(1)} %fusion.12, f32[4]{0:T(128)S(1)} %compare_select_fusion.2, bf16[4,32,96,1,128]{2,1,0,4,3:T(8,128)(2,1)S(1)} %copy-done.1, bf16[64,96,1,128]{1,0,3,2:T(8,128)(2,1)} %copy-done.2), kind=kOutput, calls=%fused_computation.15 | convolution fusion | flops 204472320 | bytes 11010064 | tf_op jit(solution)/shard_map/iwf,kjwf->kijf/dot_general | solution.py:63
  350.4 8.6 %pad_maximum_fusion = bf16[4,64,32,2,128]{1,2,0,4,3:T(8,128)(2,1)} fusion(bf16[4,64,32,1,128]{1,2,0,4,3:T(8,128)(2,1)} %fusion.9, bf16[4,64,32,1,128]{1,2,0,4,3:T(8,128)(2,1)} %fusion.8), kind=kLoop, calls=%fused_computation.8 | loop fusion | flops 2097152 | bytes 8388608 | tf_op jit(solution)/shard_map/stack | solution.py:70
  359.0 14.2 %copy.49 = bf16[4,64,32,2,128]{4,3,2,1,0:T(2,128)(2,1)} copy(bf16[4,64,32,2,128]{1,2,0,4,3:T(8,128)(2,1)} %pad_maximum_fusion) | data formatting | bytes 8388608 | tf_op jit(solution)/shard_map/stack | solution.py:70
  373.2 5.5 %convolution_convert_fusion = bf16[8192,256]{1,0:T(8,128)(2,1)} fusion(bf16[1024,8,2,128]{3,2,1,0:T(2,128)(2,1)} %bitcast.74, bf16[128,256]{1,0:T(8,128)(2,1)S(1)} %get-tuple-element.10, bf16[128,256]{1,0:T(8,128)(2,1)S(1)} %get-tuple-element.9), kind=kOutput, calls=%fused_computation.1 | convolution fusion | flops 1076101120 | bytes 8519680 | tf_op jit(solution)/shard_map/dot_general | solution.py:103
  (46 shorter events, 27.4 us)
Async XLA Ops:
  34.0 20.1 %copy-start.5 = (f32[201]{0:T(256)S(1)}, f32[201]{0:T(256)}, u32[]{:S(2)}) copy-start(f32[201]{0:T(256)} %param.5) | copy-start | bytes 2416
  34.0 24.8 %collective-permute-start = (bf16[2048,200]{0,1:T(8,128)(2,1)}, bf16[2048,200]{0,1:T(8,128)(2,1)}, u32[]{:S(2)}, u32[]{:S(2)}) collective-permute-start(bf16[2048,200]{0,1:T(8,128)(2,1)} %bitcast), channel_id=1, source_target_pairs={{0,8},{8,16},{16,24},{24,32},{32,40},{40,48},{48,56},{56,64},{64,7... | collective-permute-start | bytes 2457608 | tf_op jit(solution)/shard_map/ppermute | solution.py:21
  75.8 11.1 %copy-start.4 = (s32[32,4]{0,1:T(4,128)S(1)}, s32[32,4]{0,1:T(4,128)}, u32[]{:S(2)}) copy-start(s32[32,4]{0,1:T(4,128)} %param.6) | copy-start | bytes 1540
  75.8 81.3 %all-to-all-start.1 = ((bf16[32,64,3,2,128]{4,1,3,2,0:T(8,128)(2,1)}), bf16[32,64,3,2,128]{4,1,3,2,0:T(8,128)(2,1)}, u32[]{:S(2)}, u32[]{:S(2)}) async-start(bf16[32,64,3,2,128]{4,1,3,2,0:T(8,128)(2,1)} %copy.45), calls=%async_computation.1 | async-start | bytes 6291456 | tf_op jit(solution)/shard_map/all_to_all | solution.py:97
  85.8 32.5 %all-gather.2.cloned.1.call-start = ((), (), s32[]{:S(2)}) async-start(), calls=%async_computation.2 | async-start | bytes 1769472 | tf_op jit(solution)/shard_map/all_gather | solution.py:93
  157.2 146.8 %all-to-all-start = ((bf16[32,128,3,2,128]{4,1,3,2,0:T(8,128)(2,1)}), bf16[32,128,3,2,128]{4,1,3,2,0:T(8,128)(2,1)}, u32[]{:S(2)}, u32[]{:S(2)}) async-start(bf16[32,128,3,2,128]{4,1,3,2,0:T(8,128)(2,1)} %copy.43), calls=%async_computation | async-start | bytes 12582912 | tf_op jit(solution)/shard_map/all_to_all | solution.py:98
  173.9 155.2 %copy-start.2 = (bf16[64,96,1,128]{1,0,3,2:T(8,128)(2,1)}, bf16[64,96,1,128]{1,0,3,2:T(8,128)(2,1)S(1)}, u32[]{:S(2)}) copy-start(bf16[64,96,1,128]{1,0,3,2:T(8,128)(2,1)S(1)} %copy.58) | copy-start | bytes 4718596
  329.1 6.8 %copy-start = (bf16[4,32,96,1,128]{2,1,0,4,3:T(8,128)(2,1)S(1)}, bf16[4,32,96,1,128]{2,1,0,4,3:T(8,128)(2,1)}, u32[]{:S(2)}) copy-start(bf16[4,32,96,1,128]{2,1,0,4,3:T(8,128)(2,1)} %copy.57) | copy-start | bytes 9437188
  329.1 6.8 %copy-start.3 = (bf16[64,96,1,128]{1,0,3,2:T(8,128)(2,1)S(1)}, bf16[64,96,1,128]{1,0,3,2:T(8,128)(2,1)}, u32[]{:S(2)}) copy-start(bf16[64,96,1,128]{1,0,3,2:T(8,128)(2,1)} %copy.56) | copy-start | bytes 4718596
  336.0 2.2 copy-start.1
Sparse Core Ops, SparseCore 0:
  88.5 29.7 all-gather.1
where the time goes:
time: 388 us; the launch traced here: 386 us
  waiting for transfers between devices  179 us (46%)
  local copies, waits for them, and re-layouts  121 us (31%)
  matrix products  36.4 us (9%)
  starting transfers between devices  23.2 us (6%)
  between operations  14.3 us (4%)
  other arithmetic  11.5 us (3%)
    all_to_all x1, waiting for transfers between devices, on_device(): lax.all_to_all(picked_sources, 'wide', split_axis=0, concat_axis=2, tiled...  125 us
    reshape x2, local copies, waits for them, and re-layouts, on_device(): records.reshape(channel_blocks * subset_channels, windows_per_shard, WLEN)  31.7 us
    all_gather x1, waiting for transfers between devices, on_device(): lax.all_gather(virtual_channels, 'narrow', axis=1, tiled=True)  30.8 us
    unnamed x20, local copies, waits for them, and re-layouts  27.4 us
    all_to_all x1, waiting for transfers between devices, on_device(): lax.all_to_all(block_spectrum, 'wide', split_axis=0, concat_axis=2, tiled...  23.3 us
    another operation x1, local copies, waits for them, and re-layouts, cross_spectra(): jnp.stack([real * scale * live, imag * scale * live], 3)  14.2 us
    dot_general x1, matrix products, on_device(): jnp.dot(whitened, dft_table(), preferred_element_type=jnp.float32)  10.7 us
    all_to_all x1, starting transfers between devices, on_device(): lax.all_to_all(block_spectrum, 'wide', split_axis=0, concat_axis=2, tiled...  9.96 us
  transfers between devices with their start and end apart: 4, of which 3 were waited for; matrix products, arithmetic and copies ran while one was open for 13% of the time, Pallas kernels for 0%

commit v1 on v0

v1 whole, which is shorter than its diff:
```python
import functools
import math

import jax
import jax.numpy as jnp
import ml_dtypes
import numpy as np
from jax import lax
from jax.experimental import pallas as pl
from jax.experimental.pallas import tpu as pltpu
from jax.sharding import PartitionSpec as P

TAPS = 201
WLEN = 512
BINS = 128
F_LO = 4
LAGS = 256
SLOTS = 4
HALF = 256
MESH = pl.DeviceIdType.MESH
BF = jnp.bfloat16
F32 = jnp.float32


def forward_table():
    times = np.arange(WLEN)[:, None]
    bins = (F_LO + np.arange(BINS))[None, :]
    angle = ((times * bins) % WLEN).astype(np.float32) * np.float32(2.0 * math.pi / WLEN)
    scale = np.float32(1.0 / math.sqrt(WLEN))
    table = np.concatenate([np.cos(angle) * scale, -np.sin(angle) * scale], 1)
    return table.astype(ml_dtypes.bfloat16)


def lag_table():
    bins = (F_LO + np.arange(BINS))[:, None]
    lags = (np.arange(LAGS) - LAGS // 2)[None, :]
    angle = ((bins * lags) % WLEN).astype(np.float32) * np.float32(2.0 * math.pi / WLEN)
    scale = np.float32(1.0 / math.sqrt(BINS))
    table = np.concatenate([np.cos(angle) * scale, -np.sin(angle) * scale], 0)
    return table.astype(ml_dtypes.bfloat16)


def dot(a, b, contract=((1,), (0,))):
    return lax.dot_general(a, b, (contract, ((), ())), preferred_element_type=F32)


NT = ((1,), (1,))
TN = ((0,), (0,))


def tables_kernel(windows, pairs_ref, counts_ref, taps_ref, toep_ref, pick_ref, scale_ref, pick):
    taps = taps_ref[...].astype(BF).astype(F32)
    width = taps.shape[1]
    rolled = pltpu.roll(jnp.broadcast_to(taps, (2 * HALF, width)), width - HALF, 1, stride=1, stride_axis=0)
    toep_ref[...] = rolled[:, :HALF].astype(BF)
    col = lax.broadcasted_iota(jnp.int32, (4, 128), 1)
    row = lax.broadcasted_iota(jnp.int32, (4, 128), 0)
    diff = col - row
    blocks = pairs_ref.shape[0]

    def fill(r, _):
        for k in range(SLOTS):
            first = pairs_ref[r, k] * 4
            pick[pl.ds(r * 16 + k * 4, 4), :] = jnp.where(diff == first, 1.0, 0.0).astype(F32)
        return 0

    lax.fori_loop(0, blocks, fill, 0)
    pick_ref[...] = pick[...].astype(BF)
    slot = lax.broadcasted_iota(jnp.int32, (8, 128), 1) // 32
    scale_ref[...] = jnp.where(slot < counts_ref[0], 1.0 / math.sqrt(windows), 0.0).astype(F32)


def spectra_kernel(
    rec_hbm, toep, fwd, fwd_t, extract, pick,
    r12, r0, s12, s0,
    rec, halo, z12, z0, vrec, p12, p0,
    load_sem, halo_sem, z_send, z_recv, p_send, p_recv, own_sem, b_send, b_recv, c_send, c_recv,
):
    wide, narrow = 32, 8
    me = lax.axis_index("wide")
    n = lax.axis_index("narrow")
    y, core = n // 2, lax.rem(n, 2)
    other = n + 1 - 2 * core
    groups = 8

    def load(g):
        return pltpu.make_async_copy(rec_hbm.at[pl.ds(g * 4, 4)], rec.at[pl.ds(g * 4, 4)], load_sem.at[g])

    for g in range(groups):
        load(g).start()

    barrier = pltpu.get_barrier_semaphore()

    def greet(o, _):
        pl.semaphore_signal(barrier, inc=1, device_id={"wide": lax.rem(me + o, wide)}, device_id_type=MESH)
        return 0

    lax.fori_loop(1, wide, greet, 0)
    y_peers = [lax.rem(y + d, 4) * 2 + core for d in range(4)]
    y_froms = [lax.rem(y + 4 - d, 4) * 2 for d in range(4)]
    for peer in y_peers[1:] + [other]:
        pl.semaphore_signal(barrier, inc=1, device_id={"narrow": peer}, device_id_type=MESH)
    pl.semaphore_wait(barrier, wide - 1 + 4)

    halo_copy = pltpu.make_async_remote_copy(
        src_ref=rec_hbm.at[:, :, pl.ds(1280, HALF)], dst_ref=halo, send_sem=halo_sem.at[0], recv_sem=halo_sem.at[1],
        device_id={"wide": lax.rem(me + 1, wide)}, device_id_type=MESH)
    halo_copy.start()

    def whiten(left, right):
        return (dot(left, toep[0:HALF, :]) + dot(right, toep[HALF:, :])).astype(BF)

    def send_sources(picked, landing, ws):
        def one(o, _):
            dst = lax.rem(me + o, wide)
            pltpu.make_async_remote_copy(
                src_ref=picked.at[dst], dst_ref=landing.at[n, me], send_sem=p_send.at[ws], recv_sem=p_recv.at[ws],
                device_id={"wide": dst}, device_id_type=MESH).start()
            return 0

        lax.fori_loop(1, wide, one, 0)
        pltpu.make_async_copy(picked.at[me], landing.at[n, me], own_sem.at[ws]).start()

    for g in range(groups):
        load(g).wait()
    for g in range(groups):
        block = rec[pl.ds(g * 4, 4)].reshape(256, 1536)
        vrec[pl.ds(g * 16, 16), :] = dot(extract[...], block).astype(BF)
    for w in (1, 2):
        parts = []
        for h in (2 * w, 2 * w + 1):
            parts.append(whiten(vrec[:, (h - 1) * HALF : h * HALF], vrec[:, h * HALF : (h + 1) * HALF]))
        v = (dot(parts[0], fwd[0:HALF, :]) + dot(parts[1], fwd[HALF:, :])).astype(BF)
        p12[:, :, (w - 1) * 256 : w * 256] = dot(pick[...], v).astype(BF).reshape(wide, 16, 256)
    send_sources(p12, s12, 0)

    left_half = lax.broadcasted_iota(jnp.int32, (128, 128), 1) < 64

    def transform(first, second, store):
        a = dot(fwd_t[:, 0:HALF], first, NT) + dot(fwd_t[:, HALF:], second, NT)
        for t in range(2):
            re, im = a[0:128, t * 128 : (t + 1) * 128], a[128:256, t * 128 : (t + 1) * 128]
            store(2 * t, jnp.where(left_half, re, pltpu.roll(im, 64, 1)).astype(BF))
            store(2 * t + 1, jnp.where(left_half, pltpu.roll(re, 64, 1), im).astype(BF))

    def send_spectra(z, landing, g, ws):
        for e in range(4):
            dst = g * 4 + e

            @pl.when(dst != me)
            def _():
                pltpu.make_async_remote_copy(
                    src_ref=z.at[dst], dst_ref=landing.at[me], send_sem=z_send.at[ws], recv_sem=z_recv.at[ws],
                    device_id={"wide": dst}, device_id_type=MESH).start()

            @pl.when(dst == me)
            def _():
                pltpu.make_async_copy(z.at[dst], landing.at[me], own_sem.at[2 + ws]).start()

    def group12(gi, _):
        g = lax.rem(me // 4 + gi, groups)
        x = rec[pl.ds(g * 4, 4)].reshape(256, 1536)
        for w in (1, 2):
            parts = []
            for h in (2 * w, 2 * w + 1):
                parts.append(whiten(x[:, (h - 1) * HALF : h * HALF], x[:, h * HALF : (h + 1) * HALF]))

            def store(e, value, w=w):
                z12[g * 4 + e, w - 1] = value

            transform(parts[0], parts[1], store)
        send_spectra(z12, r12, g, 0)
        return 0

    lax.fori_loop(0, groups, group12, 0)

    halo_copy.wait()
    later = jnp.where(me > 0, 1.0, 0.0).astype(BF)
    for g in range(groups):
        block = halo[pl.ds(g * 4, 4)].reshape(256, HALF)
        vrec[pl.ds(g * 16, 16), 2 * HALF : 3 * HALF] = dot(extract[...], block).astype(BF)
    first = whiten(vrec[:, 2 * HALF : 3 * HALF] * later, vrec[:, 0:HALF])
    second = whiten(vrec[:, 0:HALF], vrec[:, HALF : 2 * HALF])
    v = (dot(first, fwd[0:HALF, :]) + dot(second, fwd[HALF:, :])).astype(BF)
    p0[...] = dot(pick[...], v).astype(BF).reshape(wide, 16, 256)
    send_sources(p0, s0, 1)

    def group0(gi, _):
        g = lax.rem(me // 4 + gi, groups)
        h = halo[pl.ds(g * 4, 4)].reshape(256, HALF) * later
        x = rec[pl.ds(g * 4, 4), :, 0 : 2 * HALF].reshape(256, 2 * HALF)

        def store(e, value):
            z0[g * 4 + e] = value

        transform(whiten(h, x[:, 0:HALF]), whiten(x[:, 0:HALF], x[:, HALF:]), store)
        send_spectra(z0, r0, g, 1)
        return 0

    lax.fori_loop(0, groups, group0, 0)

    def arrived(landing, ws):
        pltpu.make_async_copy(landing.at[0, pl.ds(0, wide - 1)], landing.at[0, pl.ds(0, wide - 1)], p_recv.at[ws]).wait()
        pltpu.make_async_copy(landing.at[0, 0], landing.at[0, 0], own_sem.at[ws]).wait()

    def to_peer(landing, d, ws):
        return pltpu.make_async_remote_copy(
            src_ref=landing.at[n], dst_ref=landing.at[n], send_sem=b_send.at[ws, d], recv_sem=b_recv.at[ws, d],
            device_id={"narrow": y_peers[d] if d else other}, device_id_type=MESH)

    def across(landing, d, ws):
        piece = y_froms[d] + core
        return pltpu.make_async_remote_copy(
            src_ref=landing.at[piece], dst_ref=landing.at[piece], send_sem=c_send.at[ws, d], recv_sem=c_recv.at[ws, d],
            device_id={"narrow": other}, device_id_type=MESH)

    for ws, landing in ((0, s12), (1, s0)):
        arrived(landing, ws)
        for d in (1, 2, 3, 0):
            to_peer(landing, d, ws).start()
    for ws, landing in ((0, s12), (1, s0)):
        for d in (1, 3, 2):
            to_peer(landing, d, ws).wait_recv()
            across(landing, d, ws).start()
    for ws, landing in ((0, s12), (1, s0)):
        for d in range(4):
            to_peer(landing, d, ws).wait_send()
        to_peer(landing, 0, ws).wait_recv()
        for d in (1, 2, 3):
            across(landing, d, ws).wait()
    for ws, (z, p) in enumerate(((z12, p12), (z0, p0))):
        for sem, buf in ((p_send, p), (z_send, z), (z_recv, z)):
            part = buf.at[pl.ds(0, wide - 1)]
            pltpu.make_async_copy(part, part, sem.at[ws]).wait()
        pltpu.make_async_copy(z.at[0], z.at[0], own_sem.at[2 + ws]).wait()


def correlate_kernel(r12, r0, s12, s0, perm, lag, scale, out, rs, ss, cross):
    wide, rows = 32, 96
    rs[0 : 64 * 128, :] = r12[...].reshape(64 * 128, 128).astype(F32)
    rs[64 * 128 :, :] = r0[...].reshape(32 * 128, 128).astype(F32)

    def prepare(d, _):
        for w in range(3):
            if w < 2:
                s, j = s12[:, d, :, w * 256 : (w + 1) * 256], d * 2 + w
            else:
                s, j = s0[:, d], 64 + d
            st = dot(s.reshape(128, 256), perm[...], TN)
            start = pl.multiple_of(j * 128, 128)
            ss[0, pl.ds(start, 128), :] = st[0:128]
            ss[1, pl.ds(start, 128), :] = st[128:256]
        return 0

    lax.fori_loop(0, wide, prepare, 0, unroll=2)

    def one_bin(f, _):
        left = rs[pl.ds(f, rows, stride=128), :].T.astype(BF)
        turned = jnp.concatenate([left[64:128], -left[0:64]], 0)
        re = ss[0, pl.ds(f, rows, stride=128), :].astype(BF)
        im = ss[1, pl.ds(f, rows, stride=128), :].astype(BF)
        value = dot(left, re) + dot(turned, im)
        cross[pl.ds(pl.multiple_of(f * 128, 128), 128), :] = value * scale[0:1, :]
        return 0

    lax.fori_loop(0, BINS, one_bin, 0, unroll=4)

    def one_channel(i, _):
        x = jnp.concatenate(
            [cross[pl.ds(i, 128, stride=128), :], cross[pl.ds(64 + i, 128, stride=128), :]], 0).astype(BF)
        out[:, i] = dot(x, lag[...], TN).astype(BF).reshape(SLOTS, 32, LAGS)
        return 0

    lax.fori_loop(0, 64, one_channel, 0, unroll=2)


def on_device(records, taps, pair_sources, pair_counts):
    blocks, channels, _ = records.shape
    any_spec = pl.BlockSpec(memory_space=pl.ANY)
    vmem = pl.BlockSpec(memory_space=pltpu.VMEM)
    smem = pl.BlockSpec(memory_space=pltpu.SMEM)
    shape = jax.ShapeDtypeStruct
    taps_row = jnp.pad(taps, (0, 1024 - TAPS)).reshape(1, 1024)
    toep, pick, scale = pl.pallas_call(
        functools.partial(tables_kernel, 96),
        out_shape=(shape((512, 256), BF), shape((512, 128), BF), shape((8, 128), F32)),
        in_specs=[smem, smem, vmem],
        out_specs=(vmem, vmem, vmem),
        scratch_shapes=[pltpu.VMEM((512, 128), F32)],
        name="tables",
    )(pair_sources, pair_counts, taps_row)
    forward = forward_table()
    extract = np.zeros((16, 256), ml_dtypes.bfloat16)
    extract[np.arange(16), np.arange(16) * 16] = 1
    perm = np.zeros((128, 128), ml_dtypes.bfloat16)
    for col in range(128):
        k, v = col // 32, col % 32
        perm[(v // 4) * 16 + k * 4 + v % 4, col] = 1
    dma = pltpu.SemaphoreType.DMA
    r12, r0, s12, s0 = pl.pallas_call(
        spectra_kernel,
        out_shape=(
            shape((32, 2, 128, 128), BF), shape((32, 128, 128), BF),
            shape((8, 32, 16, 512), BF), shape((8, 32, 16, 256), BF)),
        in_specs=[any_spec, vmem, vmem, vmem, vmem, vmem],
        out_specs=(any_spec,) * 4,
        scratch_shapes=[
            pltpu.VMEM((blocks, channels, 1536), BF), pltpu.VMEM((blocks, channels, HALF), BF),
            pltpu.VMEM((32, 2, 128, 128), BF), pltpu.VMEM((32, 128, 128), BF),
            pltpu.VMEM((128, 1536), BF),
            pltpu.VMEM((32, 16, 512), BF), pltpu.VMEM((32, 16, 256), BF),
            dma((8,)), dma((2,)), dma((2,)), dma((2,)), dma((2,)), dma((2,)), dma((4,)),
            dma((2, 4)), dma((2, 4)), dma((2, 4)), dma((2, 4))],
        compiler_params=pltpu.CompilerParams(collective_id=0, has_side_effects=True, vmem_limit_bytes=40 << 20),
        name="spectra",
    )(records, toep, jnp.asarray(forward), jnp.asarray(forward.T), jnp.asarray(extract), pick)
    out = pl.pallas_call(
        correlate_kernel,
        out_shape=shape((SLOTS, channels, 32, LAGS), BF),
        in_specs=[vmem] * 7,
        out_specs=vmem,
        scratch_shapes=[
            pltpu.VMEM((96 * 128, 128), F32), pltpu.VMEM((2, 96 * 128, 128), F32), pltpu.VMEM((128 * 128, 128), F32)],
        compiler_params=pltpu.CompilerParams(vmem_limit_bytes=56 << 20),
        name="correlate",
    )(r12, r0, s12, s0, jnp.asarray(perm), jnp.asarray(lag_table()), scale)
    return out[None]


def solution(mesh):
    return jax.shard_map(
        on_device,
        mesh=mesh,
        in_specs=(P(None, "narrow", "wide"), P(), P(), P("wide")),
        out_specs=P("wide", None, "narrow", None, None),
        check_vma=False,
    )
```

time: 388 us -> 173 us (0.45)
  waiting for transfers between devices: 179 us -> 0 us
  Pallas kernels: 0 us -> 157 us
  local copies, waits for them, and re-layouts: 121 us -> 12.8 us
  matrix products: 36.4 us -> 0 us
  starting transfers between devices: 23.2 us -> 0 us
  between operations: 14.3 us -> 0.68 us
  other arithmetic: 11.5 us -> 0 us
    pallas_call x0 -> x3, Pallas kernels: none -> 157 us  [the longest x1 117 us: on_device(): pl.pallas_call(spectra_kernel, out_shape=(shape((32, 2, 128, 128), BF), s...]
    all_to_all x2 -> x0, waiting for transfers between devices: 149 us -> none  [the longest x1 125 us: on_device(): lax.all_to_all(picked_sources, 'wide', split_axis=0, concat_axis=2, tiled...]
    reshape x6 -> x0, local copies, waits for them, and re-layouts: 40.1 us -> none  [the longest x2 31.7 us: on_device(): records.reshape(channel_blocks * subset_channels, windows_per_shard, WLEN)]
    dot_general x6 -> x0, matrix products: 36.4 us -> none  [the longest x1 10.7 us: on_device(): jnp.dot(whitened, dft_table(), preferred_element_type=jnp.float32)]
    all_gather x1 -> x0, waiting for transfers between devices: 30.8 us -> none  [on_device(): lax.all_gather(virtual_channels, 'narrow', axis=1, tiled=True)]
    slice x7 -> x0, local copies, waits for them, and re-layouts: 23.1 us -> none  [the longest x2 8.86 us: on_device(): history = shifted(tails[:, windows_per_shard - 1], 'wide', 1)]
    all_to_all x2 -> x0, starting transfers between devices: 17.5 us -> none  [the longest x1 9.96 us: on_device(): lax.all_to_all(block_spectrum, 'wide', split_axis=0, concat_axis=2, tiled...]
    unnamed x20 -> x19, local copies, waits for them, and re-layouts: 27.4 us -> 11.5 us
  transfers between devices with their start and end apart: 4 -> 0, of which waited for: 3 -> 0; matrix products, arithmetic and copies ran while one was open for 13% -> 0% of each run, Pallas kernels for 0% -> 0%
where the time goes in v1:
time: 173 us; the launch traced here: 170 us
  Pallas kernels  157 us (91%)
  local copies, waits for them, and re-layouts  12.8 us (7%)
    pallas_call x1, Pallas kernels, on_device(): pl.pallas_call(spectra_kernel, out_shape=(shape((32, 2, 128, 128), BF), s...  117 us
    pallas_call x1, Pallas kernels, on_device(): pl.pallas_call(correlate_kernel, out_shape=shape((SLOTS, channels, 32, LA...  37.4 us
    unnamed x19, local copies, waits for them, and re-layouts  11.5 us

profile of v1, /device:TPU:1, one launch (start us, length us, event | category | flops | bytes accessed | tf_op | source)
XLA Modules:
  0.0 170.1 jit_solution(5792123972853515474)
XLA Ops:
  0.7 1.3 pad.4
  1.9 1.4 copy.10.pairs_ref
  3.3 2.0 %tables.1 = (bf16[512,256]{1,0:T(8,128)(2,1)}, bf16[512,128]{1,0:T(8,128)(2,1)}, f32[8,128]{1,0:T(8,128)}) custom-call(s32[32,4]{1,0:T(8,128)} %copy.10.pairs_ref, s32[1]{0:T(128)S(6)} %copy.11.counts_ref, f32[1,1024]{1,0:T(1,128)} %bitcast.2), custom_call_target="tpu_custom_call" | custom-call | tf_op jit(solution)/shard_map/tables/pallas_call | solution.py:284
  5.3 0.0 copy-start.4
  5.3 0.9 copy-done.4
  6.3 0.0 copy-start.5
  6.3 0.9 copy-done.5
  7.2 0.0 copy-start.6
  7.2 0.9 copy-done.6
  8.2 0.0 copy-start.7
  8.2 0.9 copy-done.7
  9.1 0.0 copy-start.8
  9.1 0.7 copy-done.8
  9.8 117.2 %spectra.1 = (bf16[32,2,128,128]{3,2,1,0:T(8,128)(2,1)S(1)}, bf16[32,128,128]{2,1,0:T(8,128)(2,1)S(1)}, bf16[8,32,16,512]{3,2,1,0:T(8,128)(2,1)S(1)}, bf16[8,32,16,256]{3,2,1,0:T(8,128)(2,1)S(1)}) custom-call(bf16[32,64,1536]{2,1,0:T(8,128)(2,1)} %rec_hbm.1, bf16[512,256]{1,0:T(8,128)(2,1)S(1)} %copy-done.6, bf16[512,256]{1,0:T(8,128)(2,1)S(1)} %copy-done.5, ...), custom_call_target="tpu_custom_call" | custom-call | tf_op jit(solution)/shard_map/spectra/pallas_call | solution.py:300
  127.0 0.0 copy-start
  127.0 1.9 %copy-done = bf16[8,32,16,512]{3,2,1,0:T(8,128)(2,1)} copy-done((bf16[8,32,16,512]{3,2,1,0:T(8,128)(2,1)}, bf16[8,32,16,512]{3,2,1,0:T(8,128)(2,1)S(1)}, u32[]{:S(2)}) %copy-start) | copy-done | bytes 4194328
  129.0 0.0 copy-start.1
  129.0 1.3 copy-done.1
  130.3 0.0 copy-start.2
  130.3 1.3 copy-done.2
  131.6 0.0 copy-start.3
  131.6 1.1 copy-done.3
  132.7 37.4 %correlate.1 = bf16[4,64,32,256]{3,2,1,0:T(8,128)(2,1)} custom-call(bf16[32,2,128,128]{3,2,1,0:T(8,128)(2,1)} %copy-done.1, bf16[32,128,128]{2,1,0:T(8,128)(2,1)} %copy-done.3, bf16[8,32,16,512]{3,2,1,0:T(8,128)(2,1)} %copy-done, bf16[8,32,16,256]{3,2,1,0:T(8,128)(2,1)} %copy-done.2, bf16[128,128]{1,0:T(8,128)(2,1)} %constant.16.clone.perm, ...), custom_call_target="tpu_custom_call" | custom-call | tf_op jit(solution)/shard_map/correlate/pallas_call | solution.py:317
Async XLA Ops:
  5.3 0.9 copy-start.4
  6.3 0.9 copy-start.5
  7.2 0.9 copy-start.6
  8.2 0.9 copy-start.7
  9.1 0.7 copy-start.8
  127.0 1.9 %copy-start = (bf16[8,32,16,512]{3,2,1,0:T(8,128)(2,1)}, bf16[8,32,16,512]{3,2,1,0:T(8,128)(2,1)S(1)}, u32[]{:S(2)}) copy-start(bf16[8,32,16,512]{3,2,1,0:T(8,128)(2,1)S(1)} %get-tuple-element.16.s12) | copy-start | bytes 12582916
  129.0 1.3 copy-start.1
  130.3 1.3 copy-start.2
  131.6 1.1 copy-start.3

commit v2 on v1

v2 whole, which is shorter than its diff:
```python
import math

import jax
import jax.numpy as jnp
import ml_dtypes
import numpy as np
from jax import lax
from jax.experimental import pallas as pl
from jax.experimental.pallas import tpu as pltpu
from jax.sharding import PartitionSpec as P

TAPS = 201
WLEN = 512
BINS = 128
F_LO = 4
LAGS = 256
SLOTS = 4
HALF = 256
PITCH = 136
CHUNKS = 4
STEP = BINS // CHUNKS
MESH = pl.DeviceIdType.MESH
BF = jnp.bfloat16
F32 = jnp.float32


def forward_table():
    times = np.arange(WLEN)[:, None]
    bins = (F_LO + np.arange(BINS))[None, :]
    angle = ((times * bins) % WLEN).astype(np.float32) * np.float32(2.0 * math.pi / WLEN)
    scale = np.float32(1.0 / math.sqrt(WLEN))
    table = np.concatenate([np.cos(angle) * scale, -np.sin(angle) * scale], 1)
    return table.astype(ml_dtypes.bfloat16)


def lag_table():
    bins = (F_LO + np.arange(BINS))[:, None]
    lags = (np.arange(LAGS) - LAGS // 2)[None, :]
    angle = ((bins * lags) % WLEN).astype(np.float32) * np.float32(2.0 * math.pi / WLEN)
    scale = np.float32(1.0 / math.sqrt(BINS))
    table = np.concatenate([np.cos(angle) * scale, -np.sin(angle) * scale], 0)
    return table.astype(ml_dtypes.bfloat16)


def dot(a, b, contract=((1,), (0,))):
    return lax.dot_general(a, b, (contract, ((), ())), preferred_element_type=F32)


NT = ((1,), (1,))
TN = ((0,), (0,))


def fill_tables(windows, taps, pairs, counts, repeat, taps_row, toep, pick, scale):
    taps_row[...] = jnp.zeros_like(taps_row)
    taps_row[:, 0:TAPS] = taps[...].astype(BF).astype(F32)
    width = taps_row.shape[1]
    rolled = pltpu.roll(
        jnp.broadcast_to(taps_row[...], (2 * HALF, width)), width - HALF, 1, stride=1, stride_axis=0)
    toep[...] = rolled[:, :HALF].astype(BF)
    every = dot(repeat[...], pairs[...].astype(F32).astype(BF), NT)
    lane = lax.broadcasted_iota(jnp.int32, (512, SLOTS), 1)
    slot = lax.rem(lax.broadcasted_iota(jnp.int32, (512, SLOTS), 0) // 4, SLOTS)
    source = jnp.sum(jnp.where(lane == slot, every, 0.0), axis=1, keepdims=True)
    col = lax.broadcasted_iota(jnp.int32, (512, 128), 1)
    row = lax.broadcasted_iota(jnp.int32, (512, 128), 0)
    same = lax.rem(col, 4) == lax.rem(row, 4)
    pick[...] = jnp.where(same & ((col // 4).astype(F32) == source), 1.0, 0.0).astype(BF)
    slot = lax.broadcasted_iota(jnp.int32, (8, 128), 1) // 32
    scale[...] = jnp.where(slot < counts[0], 1.0 / math.sqrt(windows), 0.0).astype(F32)


def whole_kernel(
    counts, rec_hbm, taps_hbm, pairs_hbm, fwd_hbm, fwd_t_hbm, extract_hbm, repeat_hbm, perm_hbm, lag_hbm,
    out_hbm,
    taps, pairs, fwd, fwd_t, extract, repeat, perm, lag, taps_row, toep, pick, scale,
    rec, halo, z12, z0, r12, r0, vrec, p12, p0, s12, s0, rs, ss, cross, out,
    const_sem, load_sem, halo_sem, z_send, z_recv, p_send, p_recv, own_sem, b_send, b_recv, c_send, c_recv, out_sem,
):
    wide, groups, rows = 32, 8, 96
    me = lax.axis_index("wide")
    n = lax.axis_index("narrow")
    y, core = n // 2, lax.rem(n, 2)
    other = n + 1 - 2 * core

    consts = [
        pltpu.make_async_copy(a, b, const_sem.at[i])
        for i, (a, b) in enumerate((
            (taps_hbm, taps), (pairs_hbm, pairs), (repeat_hbm, repeat), (extract_hbm, extract),
            (fwd_hbm, fwd), (fwd_t_hbm, fwd_t), (perm_hbm, perm), (lag_hbm, lag)))
    ]

    def load(g):
        return pltpu.make_async_copy(rec_hbm.at[pl.ds(g * 4, 4)], rec.at[pl.ds(g * 4, 4)], load_sem.at[g])

    for c in consts:
        c.start()
    for g in range(groups):
        load(g).start()

    barrier = pltpu.get_barrier_semaphore()

    def greet(o, _):
        pl.semaphore_signal(barrier, inc=1, device_id={"wide": lax.rem(me + o, wide)}, device_id_type=MESH)
        return 0

    lax.fori_loop(1, wide, greet, 0)
    y_peers = [lax.rem(y + d, 4) * 2 + core for d in range(4)]
    y_froms = [lax.rem(y + 4 - d, 4) * 2 for d in range(4)]
    for peer in y_peers[1:] + [other]:
        pl.semaphore_signal(barrier, inc=1, device_id={"narrow": peer}, device_id_type=MESH)

    for c in consts:
        c.wait()
    fill_tables(rows, taps, pairs, counts, repeat, taps_row, toep, pick, scale)
    pl.semaphore_wait(barrier, wide - 1 + 4)

    halo_copy = pltpu.make_async_remote_copy(
        src_ref=rec_hbm.at[:, :, pl.ds(1280, HALF)], dst_ref=halo, send_sem=halo_sem.at[0], recv_sem=halo_sem.at[1],
        device_id={"wide": lax.rem(me + 1, wide)}, device_id_type=MESH)
    halo_copy.start()

    def whiten(left, right):
        return (dot(left, toep[0:HALF, :]) + dot(right, toep[HALF:, :])).astype(BF)

    def send_sources(picked, landing, ws):
        def one(o, _):
            dst = lax.rem(me + o, wide)
            pltpu.make_async_remote_copy(
                src_ref=picked.at[dst], dst_ref=landing.at[n, me], send_sem=p_send.at[ws], recv_sem=p_recv.at[ws],
                device_id={"wide": dst}, device_id_type=MESH).start()
            return 0

        lax.fori_loop(1, wide, one, 0)
        pltpu.make_async_copy(picked.at[me], landing.at[n, me], own_sem.at[ws]).start()

    for g in range(groups):
        load(g).wait()
        block = rec[pl.ds(g * 4, 4)].reshape(256, 1536)
        vrec[pl.ds(g * 16, 16), :] = dot(extract[...], block).astype(BF)
    for w in (1, 2):
        parts = []
        for h in (2 * w, 2 * w + 1):
            parts.append(whiten(vrec[:, (h - 1) * HALF : h * HALF], vrec[:, h * HALF : (h + 1) * HALF]))
        v = (dot(parts[0], fwd[0:HALF, :]) + dot(parts[1], fwd[HALF:, :])).astype(BF)
        p12[:, :, (w - 1) * 256 : w * 256] = dot(pick[...], v).astype(BF).reshape(wide, 16, 256)
    send_sources(p12, s12, 0)

    left_half = lax.broadcasted_iota(jnp.int32, (128, 128), 1) < 64

    def transform(first, second, store):
        a = dot(fwd_t[:, 0:HALF], first, NT) + dot(fwd_t[:, HALF:], second, NT)
        for t in range(2):
            re, im = a[0:128, t * 128 : (t + 1) * 128], a[128:256, t * 128 : (t + 1) * 128]
            store(2 * t, jnp.where(left_half, re, pltpu.roll(im, 64, 1)).astype(BF))
            store(2 * t + 1, jnp.where(left_half, pltpu.roll(re, 64, 1), im).astype(BF))

    def piece(ref, lead, c):
        at = pl.ds(pl.multiple_of(c * STEP, STEP), STEP)
        return ref.at[lead, :, at] if len(ref.shape) == 4 else ref.at[lead, at]

    def send_piece(z, landing, dst, ws, c):
        pltpu.make_async_remote_copy(
            src_ref=piece(z, dst, c), dst_ref=piece(landing, me, c),
            send_sem=z_send.at[ws, c], recv_sem=z_recv.at[ws, c],
            device_id={"wide": dst}, device_id_type=MESH).start()

    def send_group(z, landing, g, ws, chunks):
        for e in range(4):
            dst = g * 4 + e

            @pl.when(dst != me)
            def _():
                for c in chunks:
                    send_piece(z, landing, dst, ws, c)

            @pl.when(dst == me)
            def _():
                pltpu.make_async_copy(z.at[dst], landing.at[me], own_sem.at[2 + ws]).start()

    def send_rest(z, landing, ws, c):
        def one(o, _):
            send_piece(z, landing, lax.rem(me + o, wide), ws, c)
            return 0

        lax.fori_loop(1, wide, one, 0)

    def group12(gi, _):
        g = lax.rem(me // 4 + gi, groups)
        x = rec[pl.ds(g * 4, 4)].reshape(256, 1536)
        for w in (1, 2):
            parts = []
            for h in (2 * w, 2 * w + 1):
                parts.append(whiten(x[:, (h - 1) * HALF : h * HALF], x[:, h * HALF : (h + 1) * HALF]))

            def store(e, value, w=w):
                z12[g * 4 + e, w - 1] = value

            transform(parts[0], parts[1], store)
        send_group(z12, r12, g, 0, (0, 1))
        return 0

    lax.fori_loop(0, groups, group12, 0)

    def arrived(landing, ws):
        some = landing.at[0, pl.ds(0, wide - 1)]
        pltpu.make_async_copy(some, some, p_recv.at[ws]).wait()
        pltpu.make_async_copy(landing.at[0, 0], landing.at[0, 0], own_sem.at[ws]).wait()

    def to_peer(landing, d, ws):
        return pltpu.make_async_remote_copy(
            src_ref=landing.at[n], dst_ref=landing.at[n], send_sem=b_send.at[ws, d], recv_sem=b_recv.at[ws, d],
            device_id={"narrow": y_peers[d] if d else other}, device_id_type=MESH)

    def across(landing, d, ws):
        part = y_froms[d] + core
        return pltpu.make_async_remote_copy(
            src_ref=landing.at[part], dst_ref=landing.at[part], send_sem=c_send.at[ws, d], recv_sem=c_recv.at[ws, d],
            device_id={"narrow": other}, device_id_type=MESH)

    def gather_start(landing, ws):
        arrived(landing, ws)
        for d in (1, 2, 3, 0):
            to_peer(landing, d, ws).start()

    def gather_across(landing, ws):
        for d in (1, 3, 2):
            to_peer(landing, d, ws).wait_recv()
            across(landing, d, ws).start()

    def gather_end(landing, ws):
        for d in range(4):
            to_peer(landing, d, ws).wait_send()
        to_peer(landing, 0, ws).wait_recv()
        for d in (1, 2, 3):
            across(landing, d, ws).wait()

    gather_start(s12, 0)

    halo_copy.wait()
    later = jnp.where(me > 0, 1.0, 0.0).astype(BF)
    for g in range(groups):
        block = halo[pl.ds(g * 4, 4)].reshape(256, HALF)
        vrec[pl.ds(g * 16, 16), 2 * HALF : 3 * HALF] = dot(extract[...], block).astype(BF)
    first = whiten(vrec[:, 2 * HALF : 3 * HALF] * later, vrec[:, 0:HALF])
    second = whiten(vrec[:, 0:HALF], vrec[:, HALF : 2 * HALF])
    v = (dot(first, fwd[0:HALF, :]) + dot(second, fwd[HALF:, :])).astype(BF)
    p0[...] = dot(pick[...], v).astype(BF).reshape(wide, 16, 256)
    send_sources(p0, s0, 1)

    def group0(gi, _):
        g = lax.rem(me // 4 + gi, groups)
        h = halo[pl.ds(g * 4, 4)].reshape(256, HALF) * later
        x = rec[pl.ds(g * 4, 4), :, 0 : 2 * HALF].reshape(256, 2 * HALF)

        def store(e, value):
            z0[g * 4 + e] = value

        transform(whiten(h, x[:, 0:HALF]), whiten(x[:, 0:HALF], x[:, HALF:]), store)
        send_group(z0, r0, g, 1, (0, 1))
        return 0

    lax.fori_loop(0, groups, group0, 0)
    for c in range(2, CHUNKS):
        send_rest(z12, r12, 0, c)
        send_rest(z0, r0, 1, c)

    def turn(s, j):
        st = dot(s.reshape(128, 256), perm[...], TN)
        start = pl.multiple_of(j * PITCH, 8)
        ss[0, pl.ds(start, 128), :] = st[0:128]
        ss[1, pl.ds(start, 128), :] = st[128:256]

    def turn12(d, _):
        for w in range(2):
            turn(s12[:, d, :, w * 256 : (w + 1) * 256], d * 2 + w)
        return 0

    def turn0(d, _):
        turn(s0[:, d], 64 + d)
        return 0

    gather_across(s12, 0)
    gather_start(s0, 1)
    gather_end(s12, 0)
    lax.fori_loop(0, wide, turn12, 0, unroll=2)
    gather_across(s0, 1)
    gather_end(s0, 1)
    lax.fori_loop(0, wide, turn0, 0, unroll=4)

    for ws, z in enumerate((z12, z0)):
        pltpu.make_async_copy(z.at[0], z.at[0], own_sem.at[2 + ws]).wait()

    def one_bin(f):
        left = rs[pl.ds(f, rows, stride=PITCH), :].T.astype(BF)
        turned = jnp.concatenate([left[64:128], -left[0:64]], 0)
        re = ss[0, pl.ds(f, rows, stride=PITCH), :].astype(BF)
        im = ss[1, pl.ds(f, rows, stride=PITCH), :].astype(BF)
        value = dot(left, re) + dot(turned, im)
        cross[pl.ds(pl.multiple_of(f * PITCH, 8), 128), :] = value * scale[0:1, :]

    def one_chunk(c, _):
        base = pl.multiple_of(c * STEP, STEP)
        for ws, landing in ((0, r12), (1, r0)):
            some = piece(landing, pl.ds(0, wide - 1), 0)
            pltpu.make_async_copy(some, some, z_recv.at[ws, c]).wait()

        def widen(d, _):
            for j, part in ((2 * d, r12.at[d, 0]), (2 * d + 1, r12.at[d, 1]), (64 + d, r0.at[d])):
                rs[pl.ds(pl.multiple_of(j * PITCH + base, 8), STEP), :] = part[pl.ds(base, STEP), :].astype(F32)
            return 0

        lax.fori_loop(0, wide, widen, 0, unroll=4)

        def some_bins(i, _):
            for u in range(16):
                one_bin(base + i * 16 + u)
            return 0

        lax.fori_loop(0, STEP // 16, some_bins, 0)
        return 0

    lax.fori_loop(0, CHUNKS, one_chunk, 0)

    def write(q):
        at = pl.ds(pl.multiple_of(q * 16, 16), 16)
        return pltpu.make_async_copy(out.at[:, at], out_hbm.at[:, at], out_sem.at[q])

    def channels(q, _):
        for u in range(16):
            i = q * 16 + u
            x = jnp.concatenate(
                [cross[pl.ds(i, 128, stride=PITCH), :], cross[pl.ds(64 + i, 128, stride=PITCH), :]], 0).astype(BF)
            out[:, i] = dot(x, lag[...], TN).astype(BF).reshape(SLOTS, 32, LAGS)
        write(q).start()
        return 0

    lax.fori_loop(0, 4, channels, 0)
    for ws, (z, p) in enumerate(((z12, p12), (z0, p0))):
        some = p.at[pl.ds(0, wide - 1)]
        pltpu.make_async_copy(some, some, p_send.at[ws]).wait()
        for c in range(CHUNKS):
            some = piece(z, pl.ds(0, wide - 1), c)
            pltpu.make_async_copy(some, some, z_send.at[ws, c]).wait()
    for q in range(4):
        write(q).wait()


def on_device(records, taps, pair_sources, pair_counts):
    blocks, channels, _ = records.shape
    any_spec = pl.BlockSpec(memory_space=pl.ANY)
    smem = pl.BlockSpec(memory_space=pltpu.SMEM)
    forward = forward_table()
    extract = np.zeros((16, 256), ml_dtypes.bfloat16)
    extract[np.arange(16), np.arange(16) * 16] = 1
    repeat = np.zeros((512, 32), ml_dtypes.bfloat16)
    repeat[np.arange(512), np.arange(512) // 16] = 1
    perm = np.zeros((128, 128), ml_dtypes.bfloat16)
    for col in range(128):
        k, v = col // 32, col % 32
        perm[(v // 4) * 16 + k * 4 + v % 4, col] = 1
    dma = pltpu.SemaphoreType.DMA
    vm = lambda *shape, dtype=BF: pltpu.VMEM(shape, dtype)
    out = pl.pallas_call(
        whole_kernel,
        out_shape=jax.ShapeDtypeStruct((SLOTS, channels, 32, LAGS), BF),
        in_specs=[smem] + [any_spec] * 9,
        out_specs=any_spec,
        scratch_shapes=[
            vm(1, TAPS, dtype=F32), vm(SLOTS, 32, dtype=jnp.int32), vm(512, 256), vm(256, 512), vm(16, 256),
            vm(512, 32), vm(128, 128), vm(256, 256), vm(1, 1024, dtype=F32), vm(512, 256), vm(512, 128),
            vm(8, 128, dtype=F32),
            vm(blocks, channels, 1536), vm(blocks, channels, HALF),
            vm(32, 2, 128, 128), vm(32, 128, 128), vm(32, 2, 128, 128), vm(32, 128, 128), vm(128, 1536),
            vm(32, 16, 512), vm(32, 16, 256), vm(8, 32, 16, 512), vm(8, 32, 16, 256),
            vm(96 * PITCH, 128, dtype=F32), vm(2, 96 * PITCH, 128, dtype=F32), vm(128 * PITCH, 128, dtype=F32),
            vm(SLOTS, channels, 32, LAGS),
            dma((8,)), dma((8,)), dma((2,)), dma((2, CHUNKS)), dma((2, CHUNKS)), dma((2,)), dma((2,)), dma((4,)),
            dma((2, 4)), dma((2, 4)), dma((2, 4)), dma((2, 4)), dma((4,))],
        compiler_params=pltpu.CompilerParams(collective_id=0, has_side_effects=True, vmem_limit_bytes=62 << 20),
        name="correlations",
    )(pair_counts, records, taps.reshape(1, TAPS), pair_sources.T, jnp.asarray(forward), jnp.asarray(forward.T),
      jnp.asarray(extract), jnp.asarray(repeat), jnp.asarray(perm), jnp.asarray(lag_table()))
    return out[None]


def solution(mesh):
    return jax.shard_map(
        on_device,
        mesh=mesh,
        in_specs=(P(None, "narrow", "wide"), P(), P(), P("wide")),
        out_specs=P("wide", None, "narrow", None, None),
        check_vma=False,
    )
```

time: 173 us -> 133 us (0.77); the launches traced: 170 us -> 132 us
  Pallas kernels: 157 us -> 127 us
  local copies, waits for them, and re-layouts: 12.8 us -> 4.64 us
    pallas_call x3 -> x1, Pallas kernels: 157 us -> 127 us  [on_device(): pl.pallas_call(whole_kernel, out_shape=jax.ShapeDtypeStruct((SLOTS, chann...]
    unnamed x19 -> x1, local copies, waits for them, and re-layouts: 11.5 us -> 4.64 us
where the time goes in v2:
time: 133 us; the launch traced here: 132 us
  Pallas kernels  127 us (95%)
  local copies, waits for them, and re-layouts  4.64 us (3%)
    pallas_call x1, Pallas kernels, on_device(): pl.pallas_call(whole_kernel, out_shape=jax.ShapeDtypeStruct((SLOTS, chann...  127 us
    unnamed x1, local copies, waits for them, and re-layouts  4.64 us

profile of v2, /device:TPU:1, one launch (start us, length us, event | category | flops | bytes accessed | tf_op | source)
XLA Modules:
  0.0 132.0 jit_solution(3643475525875277167)
XLA Ops:
  0.7 126.7 %correlations.1 = bf16[4,64,32,256]{3,2,1,0:T(8,128)(2,1)} custom-call(s32[1]{0:T(128)S(6)} %copy.12.counts, bf16[32,64,1536]{2,1,0:T(8,128)(2,1)} %rec_hbm.1, f32[1,201]{1,0:T(1,128)} %bitcast.5, s32[4,32]{1,0:T(4,128)} %bitcast.4, bf16[512,256]{1,0:T(8,128)(2,1)} %constant.12.clone.fwd_hbm, bf16[256,512]{1,0:T(8,128)(2,1)} %constant.13.clone.fwd_t_hbm, ...), custom_call_target="tpu_custom_call" | custom-call | tf_op jit(solution)/shard_map/correlations/pallas_call | solution.py:363
  127.3 4.6 %copy.13 = bf16[1,4,64,32,256]{4,3,2,1,0:T(8,128)(2,1)} copy(bf16[1,4,64,32,256]{4,3,2,1,0:T(8,128)(2,1)} %bitcast.3) | data formatting | bytes 8388608

commit v3 on v2

--- a/solution.py
+++ b/solution.py
@@ -17,8 +17,9 @@
 SLOTS = 4
 HALF = 256
 PITCH = 136
-CHUNKS = 4
-STEP = BINS // CHUNKS
+PAST = 208
+FIRST = 2
+CHUNKS = ((0, 112), (112, 16))
 MESH = pl.DeviceIdType.MESH
 BF = jnp.bfloat16
 F32 = jnp.float32
@@ -70,11 +71,11 @@
 
 
 def whole_kernel(
-    counts, rec_hbm, taps_hbm, pairs_hbm, fwd_hbm, fwd_t_hbm, extract_hbm, repeat_hbm, perm_hbm, lag_hbm,
-    out_hbm,
-    taps, pairs, fwd, fwd_t, extract, repeat, perm, lag, taps_row, toep, pick, scale,
-    rec, halo, z12, z0, r12, r0, vrec, p12, p0, s12, s0, rs, ss, cross, out,
-    const_sem, load_sem, halo_sem, z_send, z_recv, p_send, p_recv, own_sem, b_send, b_recv, c_send, c_recv, out_sem,
+    counts, rec_hbm, taps_hbm, pairs_hbm, fwd_hbm, fwd_t_hbm, extract_hbm, repeat_hbm, perm_hbm, shift_hbm,
+    out,
+    taps, pairs, fwd, fwd_t, extract, repeat, perm, shift, taps_row, toep, pick, scale,
+    rec, own_past, past, past_source, z12, z0, r12, r0, vrec, p12, p0, s12, s0, rs, ss, cross, turned_cross, relay,
+    const_sem, load_sem, halo_sem, z_send, z_recv, p_send, p_recv, own_sem, b_send, b_recv, c_send, c_recv, relay_sem, onward_sem, out_sem,
 ):
     wide, groups, rows = 32, 8, 96
     me = lax.axis_index("wide")
@@ -86,16 +87,26 @@
         pltpu.make_async_copy(a, b, const_sem.at[i])
         for i, (a, b) in enumerate((
             (taps_hbm, taps), (pairs_hbm, pairs), (repeat_hbm, repeat), (extract_hbm, extract),
-            (fwd_hbm, fwd), (fwd_t_hbm, fwd_t), (perm_hbm, perm), (lag_hbm, lag)))
+            (shift_hbm, shift), (fwd_hbm, fwd), (fwd_t_hbm, fwd_t), (perm_hbm, perm)))
     ]
 
     def load(g):
-        return pltpu.make_async_copy(rec_hbm.at[pl.ds(g * 4, 4)], rec.at[pl.ds(g * 4, 4)], load_sem.at[g])
+        part = (pl.ds(g * 4, 4), slice(None), pl.ds(0, 1280))
+        return pltpu.make_async_copy(rec_hbm.at[part], rec.at[part], load_sem.at[g])
+
+    last = (slice(None), slice(None), pl.ds(1280, HALF))
+    tails = pltpu.make_async_copy(rec_hbm.at[last], rec.at[last], load_sem.at[groups])
+    tails.start()
 
     for c in consts:
         c.start()
-    for g in range(groups):
-        load(g).start()
+    x, z_at = me // 8, lax.rem(me, 8)
+
+    def group_at(gi):
+        return lax.rem(x + gi, 4) * 2 + lax.rem(z_at // 4 + 1 + gi // 4, 2)
+
+    for gi in range(groups):
+        load(group_at(gi)).start()
 
     barrier = pltpu.get_barrier_semaphore()
 
@@ -112,12 +123,11 @@
     for c in consts:
         c.wait()
     fill_tables(rows, taps, pairs, counts, repeat, taps_row, toep, pick, scale)
-    pl.semaphore_wait(barrier, wide - 1 + 4)
-
-    halo_copy = pltpu.make_async_remote_copy(
-        src_ref=rec_hbm.at[:, :, pl.ds(1280, HALF)], dst_ref=halo, send_sem=halo_sem.at[0], recv_sem=halo_sem.at[1],
-        device_id={"wide": lax.rem(me + 1, wide)}, device_id_type=MESH)
-    halo_copy.start()
+
+    tails.wait()
+    for g in range(groups):
+        tail = rec[pl.ds(g * 4, 4), :, 1280:].reshape(256, HALF)
+        own_past[:, g * 256 : (g + 1) * 256] = dot(shift[...], tail, NT).astype(BF)
 
     def whiten(left, right):
         return (dot(left, toep[0:HALF, :]) + dot(right, toep[HALF:, :])).astype(BF)
@@ -133,8 +143,104 @@
         lax.fori_loop(1, wide, one, 0)
         pltpu.make_async_copy(picked.at[me], landing.at[n, me], own_sem.at[ws]).start()
 
+    left_half = lax.broadcasted_iota(jnp.int32, (128, 128), 1) < 64
+
+    def transform(first, second, store):
+        a = dot(fwd_t[:, 0:HALF], first, NT) + dot(fwd_t[:, HALF:], second, NT)
+        for t in range(2):
+            re, im = a[0:128, t * 128 : (t + 1) * 128], a[128:256, t * 128 : (t + 1) * 128]
+            store(2 * t, jnp.where(left_half, re, pltpu.roll(im, 64, 1)).astype(BF))
+            store(2 * t + 1, jnp.where(left_half, pltpu.roll(re, 64, 1), im).astype(BF))
+
+    def piece(ref, lead, c):
+        at = pl.ds(*CHUNKS[c])
+        return ref.at[lead, :, at] if len(ref.shape) == 4 else ref.at[lead, at]
+
+    def send_piece(z, landing, dst, ws, c):
+        pltpu.make_async_remote_copy(
+            src_ref=piece(z, dst, c), dst_ref=piece(landing, me, c),
+            send_sem=z_send.at[ws, c], recv_sem=z_recv.at[ws, c],
+            device_id={"wide": dst}, device_id_type=MESH).start()
+
+    half_way, relay_to = lax.rem(z_at + 4, 8), x * 8 + lax.rem(z_at + 6, 8)
+
+    def send_group(z, landing, g, ws):
+        for e in range(4):
+            dst = g * 4 + e
+            far = (lax.rem(dst, 8) == half_way) if ws == 0 else False
+
+            @pl.when((dst != me) & jnp.logical_not(far))
+            def _():
+                send_piece(z, landing, dst, ws, 0)
+
+            if ws == 0:
+
+                @pl.when(far)
+                def _():
+                    pltpu.make_async_remote_copy(
+                        src_ref=piece(z, dst, 0), dst_ref=relay.at[lax.rem(dst // 8 + 4 - x, 4)],
+                        send_sem=z_send.at[ws, 0], recv_sem=relay_sem,
+                        device_id={"wide": relay_to}, device_id_type=MESH).start()
+
+            @pl.when(dst == me)
+            def _():
+                pltpu.make_async_copy(z.at[dst], landing.at[me], own_sem.at[2 + ws]).start()
+
+    def onward():
+        pltpu.make_async_copy(relay, relay, relay_sem).wait()
+        origin = x * 8 + lax.rem(z_at + 2, 8)
+        for d in range(4):
+            pltpu.make_async_remote_copy(
+                src_ref=relay.at[d], dst_ref=piece(r12, origin, 0),
+                send_sem=onward_sem, recv_sem=z_recv.at[0, 0],
+                device_id={"wide": lax.rem(x + d, 4) * 8 + lax.rem(z_at + 6, 8)}, device_id_type=MESH).start()
+
+    def send_rest(z, landing, ws, c):
+        def one(o, _):
+            send_piece(z, landing, lax.rem(me + o, wide), ws, c)
+            return 0
+
+        lax.fori_loop(1, wide, one, 0)
+
+    def group12(gi, _):
+        g = group_at(gi)
+        x = rec[pl.ds(g * 4, 4)].reshape(256, 1536)
+        for w in (1, 2):
+            parts = []
+            for h in (2 * w, 2 * w + 1):
+                parts.append(whiten(x[:, (h - 1) * HALF : h * HALF], x[:, h * HALF : (h + 1) * HALF]))
+
+            def store(e, value, w=w):
+                z12[g * 4 + e, w - 1] = value
+
+            transform(parts[0], parts[1], store)
+        return 0
+
+    def next12(gi, _):
+        group12(gi, 0)
+        return send12(gi, 0)
+
+    def first12(gi, _):
+        load(group_at(gi)).wait()
+        return group12(gi, 0)
+
+    lax.fori_loop(0, FIRST, first12, 0)
+
+    pl.semaphore_wait(barrier, wide - 1 + 4)
+    past_copy = pltpu.make_async_remote_copy(
+        src_ref=own_past, dst_ref=past, send_sem=halo_sem.at[0], recv_sem=halo_sem.at[1],
+        device_id={"wide": lax.rem(me + 1, wide)}, device_id_type=MESH)
+    past_copy.start()
+
+    def send12(gi, _):
+        send_group(z12, r12, group_at(gi), 0)
+        return 0
+
+    lax.fori_loop(0, FIRST, send12, 0)
+
+    for gi in range(FIRST, groups):
+        load(group_at(gi)).wait()
     for g in range(groups):
-        load(g).wait()
         block = rec[pl.ds(g * 4, 4)].reshape(256, 1536)
         vrec[pl.ds(g * 16, 16), :] = dot(extract[...], block).astype(BF)
     for w in (1, 2):
@@ -145,61 +251,7 @@
         p12[:, :, (w - 1) * 256 : w * 256] = dot(pick[...], v).astype(BF).reshape(wide, 16, 256)
     send_sources(p12, s12, 0)
 
-    left_half = lax.broadcasted_iota(jnp.int32, (128, 128), 1) < 64
-
-    def transform(first, second, store):
-        a = dot(fwd_t[:, 0:HALF], first, NT) + dot(fwd_t[:, HALF:], second, NT)
-        for t in range(2):
-            re, im = a[0:128, t * 128 : (t + 1) * 128], a[128:256, t * 128 : (t + 1) * 128]
-            store(2 * t, jnp.where(left_half, re, pltpu.roll(im, 64, 1)).astype(BF))
-            store(2 * t + 1, jnp.where(left_half, pltpu.roll(re, 64, 1), im).astype(BF))
-
-    def piece(ref, lead, c):
-        at = pl.ds(pl.multiple_of(c * STEP, STEP), STEP)
-        return ref.at[lead, :, at] if len(ref.shape) == 4 else ref.at[lead, at]
-
-    def send_piece(z, landing, dst, ws, c):
-        pltpu.make_async_remote_copy(
-            src_ref=piece(z, dst, c), dst_ref=piece(landing, me, c),
-            send_sem=z_send.at[ws, c], recv_sem=z_recv.at[ws, c],
-            device_id={"wide": dst}, device_id_type=MESH).start()
-
-    def send_group(z, landing, g, ws, chunks):
-        for e in range(4):
-            dst = g * 4 + e
-
-            @pl.when(dst != me)
-            def _():
-                for c in chunks:
-                    send_piece(z, landing, dst, ws, c)
-
-            @pl.when(dst == me)
-            def _():
-                pltpu.make_async_copy(z.at[dst], landing.at[me], own_sem.at[2 + ws]).start()
-
-    def send_rest(z, landing, ws, c):
-        def one(o, _):
-            send_piece(z, landing, lax.rem(me + o, wide), ws, c)
-            return 0
-
-        lax.fori_loop(1, wide, one, 0)
-
-    def group12(gi, _):
-        g = lax.rem(me // 4 + gi, groups)
-        x = rec[pl.ds(g * 4, 4)].reshape(256, 1536)
-        for w in (1, 2):
-            parts = []
-            for h in (2 * w, 2 * w + 1):
-                parts.append(whiten(x[:, (h - 1) * HALF : h * HALF], x[:, h * HALF : (h + 1) * HALF]))
-
-            def store(e, value, w=w):
-                z12[g * 4 + e, w - 1] = value
-
-            transform(parts[0], parts[1], store)
-        send_group(z12, r12, g, 0, (0, 1))
-        return 0
-
-    lax.fori_loop(0, groups, group12, 0)
+    lax.fori_loop(FIRST, groups, next12, 0)
 
     def arrived(landing, ws):
         some = landing.at[0, pl.ds(0, wide - 1)]
@@ -234,35 +286,39 @@
         for d in (1, 2, 3):
             across(landing, d, ws).wait()
 
-    gather_start(s12, 0)
-
-    halo_copy.wait()
-    later = jnp.where(me > 0, 1.0, 0.0).astype(BF)
+    onward()
+
+    past_copy.wait()
+    later = jnp.where(me > 0, 1.0, 0.0).astype(F32)
+
+    def whiten_past(left, right, contract):
+        return (dot(left, toep[HALF - PAST : HALF, :], contract) * later + dot(right, toep[HALF:, :])).astype(BF)
+
     for g in range(groups):
-        block = halo[pl.ds(g * 4, 4)].reshape(256, HALF)
-        vrec[pl.ds(g * 16, 16), 2 * HALF : 3 * HALF] = dot(extract[...], block).astype(BF)
-    first = whiten(vrec[:, 2 * HALF : 3 * HALF] * later, vrec[:, 0:HALF])
+        block = past[:, g * 256 : (g + 1) * 256]
+        past_source[pl.ds(g * 16, 16), 0:PAST] = dot(extract[...], block, NT).astype(BF)
+    first = whiten_past(past_source[:, 0:PAST], vrec[:, 0:HALF], ((1,), (0,)))
     second = whiten(vrec[:, 0:HALF], vrec[:, HALF : 2 * HALF])
     v = (dot(first, fwd[0:HALF, :]) + dot(second, fwd[HALF:, :])).astype(BF)
     p0[...] = dot(pick[...], v).astype(BF).reshape(wide, 16, 256)
     send_sources(p0, s0, 1)
 
     def group0(gi, _):
-        g = lax.rem(me // 4 + gi, groups)
-        h = halo[pl.ds(g * 4, 4)].reshape(256, HALF) * later
+        g = group_at(gi)
+        h = past[:, pl.ds(pl.multiple_of(g * 256, 256), 256)]
         x = rec[pl.ds(g * 4, 4), :, 0 : 2 * HALF].reshape(256, 2 * HALF)
 
         def store(e, value):
             z0[g * 4 + e] = value
 
-        transform(whiten(h, x[:, 0:HALF]), whiten(x[:, 0:HALF], x[:, HALF:]), store)
-        send_group(z0, r0, g, 1, (0, 1))
+        transform(whiten_past(h, x[:, 0:HALF], TN), whiten(x[:, 0:HALF], x[:, HALF:]), store)
+        send_group(z0, r0, g, 1)
         return 0
 
     lax.fori_loop(0, groups, group0, 0)
-    for c in range(2, CHUNKS):
-        send_rest(z12, r12, 0, c)
-        send_rest(z0, r0, 1, c)
+    send_rest(z12, r12, 0, 1)
+    send_rest(z0, r0, 1, 1)
+    gather_start(s12, 0)
 
     def turn(s, j):
         st = dot(s.reshape(128, 256), perm[...], TN)
@@ -298,50 +354,72 @@
         value = dot(left, re) + dot(turned, im)
         cross[pl.ds(pl.multiple_of(f * PITCH, 8), 128), :] = value * scale[0:1, :]
 
-    def one_chunk(c, _):
-        base = pl.multiple_of(c * STEP, STEP)
+    def write(c):
+        at = pl.ds(*CHUNKS[c])
+        return pltpu.make_async_copy(turned_cross.at[:, :, at], out.at[:, :, at], out_sem.at[c])
+
+    for c, (base, step) in enumerate(CHUNKS):
         for ws, landing in ((0, r12), (1, r0)):
-            some = piece(landing, pl.ds(0, wide - 1), 0)
+            some = piece(landing, pl.ds(0, wide - 1), c)
             pltpu.make_async_copy(some, some, z_recv.at[ws, c]).wait()
 
-        def widen(d, _):
+        def widen(d, _, base=base, step=step):
             for j, part in ((2 * d, r12.at[d, 0]), (2 * d + 1, r12.at[d, 1]), (64 + d, r0.at[d])):
-                rs[pl.ds(pl.multiple_of(j * PITCH + base, 8), STEP), :] = part[pl.ds(base, STEP), :].astype(F32)
+                rs[pl.ds(pl.multiple_of(j * PITCH + base, 8), step), :] = part[base : base + step, :].astype(F32)
             return 0
 
         lax.fori_loop(0, wide, widen, 0, unroll=4)
 
-        def some_bins(i, _):
+        def some_bins(i, _, base=base):
             for u in range(16):
                 one_bin(base + i * 16 + u)
             return 0
 
-        lax.fori_loop(0, STEP // 16, some_bins, 0)
-        return 0
-
-    lax.fori_loop(0, CHUNKS, one_chunk, 0)
-
-    def write(q):
-        at = pl.ds(pl.multiple_of(q * 16, 16), 16)
-        return pltpu.make_async_copy(out.at[:, at], out_hbm.at[:, at], out_sem.at[q])
-
-    def channels(q, _):
-        for u in range(16):
-            i = q * 16 + u
-            x = jnp.concatenate(
-                [cross[pl.ds(i, 128, stride=PITCH), :], cross[pl.ds(64 + i, 128, stride=PITCH), :]], 0).astype(BF)
-            out[:, i] = dot(x, lag[...], TN).astype(BF).reshape(SLOTS, 32, LAGS)
-        write(q).start()
-        return 0
-
-    lax.fori_loop(0, 4, channels, 0)
+        lax.fori_loop(0, step // 16, some_bins, 0)
+        def regroup(i, _, base=base, step=step):
+            for p in range(2):
+                rows_of = cross[pl.ds(base * PITCH + p * 64 + i, step, stride=PITCH), :]
+                turned_cross[i, p, base : base + step, :] = rows_of.astype(BF)
+            return 0
+
+        lax.fori_loop(0, 64, regroup, 0, unroll=8)
+        write(c).start()
+
+    pltpu.make_async_copy(relay, relay, onward_sem).wait()
     for ws, (z, p) in enumerate(((z12, p12), (z0, p0))):
         some = p.at[pl.ds(0, wide - 1)]
         pltpu.make_async_copy(some, some, p_send.at[ws]).wait()
-        for c in range(CHUNKS):
+        for c in range(len(CHUNKS)):
             some = piece(z, pl.ds(0, wide - 1), c)
             pltpu.make_async_copy(some, some, z_send.at[ws, c]).wait()
-    for q in range(4):
+    for c in range(len(CHUNKS)):
+        write(c).wait()
+
+
+def lag_kernel(cross_hbm, lag_hbm, out_hbm, cross, lag, out, lag_sem, read_sem, write_sem):
+    channels, parts = cross.shape[0], 4
+    each = channels // parts
+
+    def read(q):
+        at = pl.ds(q * each, each)
+        return pltpu.make_async_copy(cross_hbm.at[at], cross.at[at], read_sem.at[q])
+
+    def write(q):
+        at = pl.ds(q * each, each)
+        return pltpu.make_async_copy(out.at[:, at], out_hbm.at[:, at], write_sem.at[q])
+
+    table = pltpu.make_async_copy(lag_hbm, lag, lag_sem)
+    table.start()
+    for q in range(parts):
+        read(q).start()
+    table.wait()
+    for q in range(parts):
+        read(q).wait()
+        for i in range(q * each, (q + 1) * each):
+            x = cross[i].reshape(2 * BINS, 128)
+            out[:, i] = dot(x, lag[...], TN).astype(BF).reshape(SLOTS, 32, LAGS)
+        write(q).start()
+    for q in range(parts):
         write(q).wait()
 
 
@@ -358,28 +436,40 @@
     for col in range(128):
         k, v = col // 32, col % 32
         perm[(v // 4) * 16 + k * 4 + v % 4, col] = 1
+    shift = np.zeros((PAST, HALF), ml_dtypes.bfloat16)
+    shift[np.arange(PAST), HALF - PAST + np.arange(PAST)] = 1
     dma = pltpu.SemaphoreType.DMA
     vm = lambda *shape, dtype=BF: pltpu.VMEM(shape, dtype)
-    out = pl.pallas_call(
+    cross = pl.pallas_call(
         whole_kernel,
-        out_shape=jax.ShapeDtypeStruct((SLOTS, channels, 32, LAGS), BF),
+        out_shape=jax.ShapeDtypeStruct((channels, 2, BINS, 128), BF),
         in_specs=[smem] + [any_spec] * 9,
         out_specs=any_spec,
         scratch_shapes=[
             vm(1, TAPS, dtype=F32), vm(SLOTS, 32, dtype=jnp.int32), vm(512, 256), vm(256, 512), vm(16, 256),
-            vm(512, 32), vm(128, 128), vm(256, 256), vm(1, 1024, dtype=F32), vm(512, 256), vm(512, 128),
+            vm(512, 32), vm(128, 128), vm(PAST, HALF), vm(1, 1024, dtype=F32), vm(512, 256), vm(512, 128),
             vm(8, 128, dtype=F32),
-            vm(blocks, channels, 1536), vm(blocks, channels, HALF),
+            vm(blocks, channels, 1536), vm(PAST, blocks * channels), vm(PAST, blocks * channels), vm(128, HALF),
             vm(32, 2, 128, 128), vm(32, 128, 128), vm(32, 2, 128, 128), vm(32, 128, 128), vm(128, 1536),
             vm(32, 16, 512), vm(32, 16, 256), vm(8, 32, 16, 512), vm(8, 32, 16, 256),
-            vm(96 * PITCH, 128, dtype=F32), vm(2, 96 * PITCH, 128, dtype=F32), vm(128 * PITCH, 128, dtype=F32),
-            vm(SLOTS, channels, 32, LAGS),
-            dma((8,)), dma((8,)), dma((2,)), dma((2, CHUNKS)), dma((2, CHUNKS)), dma((2,)), dma((2,)), dma((4,)),
-            dma((2, 4)), dma((2, 4)), dma((2, 4)), dma((2, 4)), dma((4,))],
+            vm(96 * PITCH, 128, dtype=F32), vm(2, 96 * PITCH, 128, dtype=F32), vm(BINS * PITCH, 128, dtype=F32),
+            vm(channels, 2, BINS, 128), vm(4, 2, CHUNKS[0][1], 128),
+            dma((8,)), dma((9,)), dma((2,)), dma((2, len(CHUNKS))), dma((2, len(CHUNKS))), dma((2,)), dma((2,)), dma((4,)),
+            dma((2, 4)), dma((2, 4)), dma((2, 4)), dma((2, 4)), dma, dma, dma((len(CHUNKS),))],
         compiler_params=pltpu.CompilerParams(collective_id=0, has_side_effects=True, vmem_limit_bytes=62 << 20),
-        name="correlations",
+        name="cross",
     )(pair_counts, records, taps.reshape(1, TAPS), pair_sources.T, jnp.asarray(forward), jnp.asarray(forward.T),
-      jnp.asarray(extract), jnp.asarray(repeat), jnp.asarray(perm), jnp.asarray(lag_table()))
+      jnp.asarray(extract), jnp.asarray(repeat), jnp.asarray(perm), jnp.asarray(shift))
+    out = pl.pallas_call(
+        lag_kernel,
+        out_shape=jax.ShapeDtypeStruct((SLOTS, channels, 32, LAGS), BF),
+        in_specs=[any_spec, any_spec],
+        out_specs=any_spec,
+        scratch_shapes=[
+            vm(channels, 2, BINS, 128), vm(2 * BINS, LAGS), vm(SLOTS, channels, 32, LAGS), dma, dma((4,)), dma((4,))],
+        compiler_params=pltpu.CompilerParams(vmem_limit_bytes=60 << 20),
+        name="lags",
+    )(cross, jnp.asarray(lag_table()))
     return out[None]
 
 

time: 133 us -> 121 us (0.910)
  Pallas kernels: 127 us -> 119 us
  local copies, waits for them, and re-layouts: 4.64 us -> 0 us
    pallas_call x1 -> x2, Pallas kernels: 127 us -> 119 us  [the longest x1 114 us: on_device(): pl.pallas_call(whole_kernel, out_shape=jax.ShapeDtypeStruct((channels, 2,...]
    unnamed x1 -> x0, local copies, waits for them, and re-layouts: 4.64 us -> none
where the time goes in v3:
time: 121 us; the launch traced here: 120 us
  Pallas kernels  119 us (98%)
    pallas_call x1, Pallas kernels, on_device(): pl.pallas_call(whole_kernel, out_shape=jax.ShapeDtypeStruct((channels, 2,...  114 us
    pallas_call x1, Pallas kernels, on_device(): pl.pallas_call(lag_kernel, out_shape=jax.ShapeDtypeStruct((SLOTS, channel...  4.86 us

profile of v3, /device:TPU:1, one launch (start us, length us, event | category | flops | bytes accessed | tf_op | source)
XLA Modules:
  0.0 119.9 jit_solution(3677800977968444430)
XLA Ops:
  0.7 114.4 %cross.1.cross_hbm = bf16[64,2,128,128]{3,2,1,0:T(8,128)(2,1)} custom-call(s32[1]{0:T(128)S(6)} %copy.12.counts, bf16[32,64,1536]{2,1,0:T(8,128)(2,1)} %rec_hbm.1, f32[1,201]{1,0:T(1,128)} %bitcast.4, s32[4,32]{1,0:T(4,128)} %bitcast.3, bf16[512,256]{1,0:T(8,128)(2,1)} %constant.14.clone.fwd_hbm, bf16[256,512]{1,0:T(8,128)(2,1)} %constant.15.clone.fwd_t_hbm, ...), custom_call_target="tpu_custom_call" | custom-call | tf_op jit(solution)/shard_map/cross/pallas_call | solution.py:443
  115.0 4.9 %lags.1 = bf16[4,64,32,256]{3,2,1,0:T(8,128)(2,1)} custom-call(bf16[64,2,128,128]{3,2,1,0:T(8,128)(2,1)} %cross.1.cross_hbm, bf16[256,256]{1,0:T(8,128)(2,1)} %constant.20.clone.lag_hbm), custom_call_target="tpu_custom_call" | custom-call | tf_op jit(solution)/shard_map/lags/pallas_call | solution.py:463

commit v4 on v3

--- a/solution.py
+++ b/solution.py
@@ -18,8 +18,8 @@
 HALF = 256
 PITCH = 136
 PAST = 208
-FIRST = 2
-CHUNKS = ((0, 112), (112, 16))
+FIRST = 1
+CHUNKS = ((0, 96), (96, 32))
 MESH = pl.DeviceIdType.MESH
 BF = jnp.bfloat16
 F32 = jnp.float32
@@ -51,13 +51,16 @@
 TN = ((0,), (0,))
 
 
-def fill_tables(windows, taps, pairs, counts, repeat, taps_row, toep, pick, scale):
+def fill_filter(taps, taps_row, toep):
     taps_row[...] = jnp.zeros_like(taps_row)
     taps_row[:, 0:TAPS] = taps[...].astype(BF).astype(F32)
     width = taps_row.shape[1]
     rolled = pltpu.roll(
         jnp.broadcast_to(taps_row[...], (2 * HALF, width)), width - HALF, 1, stride=1, stride_axis=0)
     toep[...] = rolled[:, :HALF].astype(BF)
+
+
+def fill_picks(windows, pairs, counts, repeat, pick, scale):
     every = dot(repeat[...], pairs[...].astype(F32).astype(BF), NT)
     lane = lax.broadcasted_iota(jnp.int32, (512, SLOTS), 1)
     slot = lax.rem(lax.broadcasted_iota(jnp.int32, (512, SLOTS), 0) // 4, SLOTS)
@@ -86,8 +89,8 @@
     consts = [
         pltpu.make_async_copy(a, b, const_sem.at[i])
         for i, (a, b) in enumerate((
-            (taps_hbm, taps), (pairs_hbm, pairs), (repeat_hbm, repeat), (extract_hbm, extract),
-            (shift_hbm, shift), (fwd_hbm, fwd), (fwd_t_hbm, fwd_t), (perm_hbm, perm)))
+            (taps_hbm, taps), (fwd_t_hbm, fwd_t), (shift_hbm, shift), (extract_hbm, extract), (pairs_hbm, pairs),
+            (repeat_hbm, repeat), (fwd_hbm, fwd), (perm_hbm, perm)))
     ]
 
     def load(g):
@@ -96,10 +99,10 @@
 
     last = (slice(None), slice(None), pl.ds(1280, HALF))
     tails = pltpu.make_async_copy(rec_hbm.at[last], rec.at[last], load_sem.at[groups])
+
+    for c in consts[0:2]:
+        c.start()
     tails.start()
-
-    for c in consts:
-        c.start()
     x, z_at = me // 8, lax.rem(me, 8)
 
     def group_at(gi):
@@ -107,6 +110,9 @@
 
     for gi in range(groups):
         load(group_at(gi)).start()
+        if gi == 0:
+            for c in consts[2:]:
+                c.start()
 
     barrier = pltpu.get_barrier_semaphore()
 
@@ -120,14 +126,9 @@
     for peer in y_peers[1:] + [other]:
         pl.semaphore_signal(barrier, inc=1, device_id={"narrow": peer}, device_id_type=MESH)
 
-    for c in consts:
+    for c in consts[0:2]:
         c.wait()
-    fill_tables(rows, taps, pairs, counts, repeat, taps_row, toep, pick, scale)
-
-    tails.wait()
-    for g in range(groups):
-        tail = rec[pl.ds(g * 4, 4), :, 1280:].reshape(256, HALF)
-        own_past[:, g * 256 : (g + 1) * 256] = dot(shift[...], tail, NT).astype(BF)
+    fill_filter(taps, taps_row, toep)
 
     def whiten(left, right):
         return (dot(left, toep[0:HALF, :]) + dot(right, toep[HALF:, :])).astype(BF)
@@ -216,6 +217,10 @@
             transform(parts[0], parts[1], store)
         return 0
 
+    def send12(gi, _):
+        send_group(z12, r12, group_at(gi), 0)
+        return 0
+
     def next12(gi, _):
         group12(gi, 0)
         return send12(gi, 0)
@@ -224,19 +229,22 @@
         load(group_at(gi)).wait()
         return group12(gi, 0)
 
+    tails.wait()
     lax.fori_loop(0, FIRST, first12, 0)
 
     pl.semaphore_wait(barrier, wide - 1 + 4)
+    lax.fori_loop(0, FIRST, send12, 0)
+
+    for c in consts[2:]:
+        c.wait()
+    for g in range(groups):
+        tail = rec[pl.ds(g * 4, 4), :, 1280:].reshape(256, HALF)
+        own_past[:, g * 256 : (g + 1) * 256] = dot(shift[...], tail, NT).astype(BF)
     past_copy = pltpu.make_async_remote_copy(
         src_ref=own_past, dst_ref=past, send_sem=halo_sem.at[0], recv_sem=halo_sem.at[1],
         device_id={"wide": lax.rem(me + 1, wide)}, device_id_type=MESH)
     past_copy.start()
-
-    def send12(gi, _):
-        send_group(z12, r12, group_at(gi), 0)
-        return 0
-
-    lax.fori_loop(0, FIRST, send12, 0)
+    fill_picks(rows, pairs, counts, repeat, pick, scale)
 
     for gi in range(FIRST, groups):
         load(group_at(gi)).wait()
@@ -286,7 +294,6 @@
         for d in (1, 2, 3):
             across(landing, d, ws).wait()
 
-    onward()
 
     past_copy.wait()
     later = jnp.where(me > 0, 1.0, 0.0).astype(F32)
@@ -315,6 +322,7 @@
         send_group(z0, r0, g, 1)
         return 0
 
+    onward()
     lax.fori_loop(0, groups, group0, 0)
     send_rest(z12, r12, 0, 1)
     send_rest(z0, r0, 1, 1)

time: 121 us -> 116 us (0.959)
  Pallas kernels: 119 us -> 115 us
    pallas_call x1, Pallas kernels: 114 us -> 111 us  [on_device(): pl.pallas_call(whole_kernel, out_shape=jax.ShapeDtypeStruct((channels, 2,...]
where the time goes in v4:
time: 116 us
  Pallas kernels  115 us (99%)
    pallas_call x1, Pallas kernels, on_device(): pl.pallas_call(whole_kernel, out_shape=jax.ShapeDtypeStruct((channels, 2,...  111 us
    pallas_call x1, Pallas kernels, on_device(): pl.pallas_call(lag_kernel, out_shape=jax.ShapeDtypeStruct((SLOTS, channel...  4.85 us

profile of v4, /device:TPU:1, one launch (start us, length us, event | category | flops | bytes accessed | tf_op | source)
XLA Modules:
  0.0 116.1 jit_solution(8093004887350427151)
XLA Ops:
  0.7 110.5 %cross.1.cross_hbm = bf16[64,2,128,128]{3,2,1,0:T(8,128)(2,1)} custom-call(s32[1]{0:T(128)S(6)} %copy.12.counts, bf16[32,64,1536]{2,1,0:T(8,128)(2,1)} %rec_hbm.1, f32[1,201]{1,0:T(1,128)} %bitcast.4, s32[4,32]{1,0:T(4,128)} %bitcast.3, bf16[512,256]{1,0:T(8,128)(2,1)} %constant.14.clone.fwd_hbm, bf16[256,512]{1,0:T(8,128)(2,1)} %constant.15.clone.fwd_t_hbm, ...), custom_call_target="tpu_custom_call" | custom-call | tf_op jit(solution)/shard_map/cross/pallas_call | solution.py:451
  111.2 4.9 %lags.1 = bf16[4,64,32,256]{3,2,1,0:T(8,128)(2,1)} custom-call(bf16[64,2,128,128]{3,2,1,0:T(8,128)(2,1)} %cross.1.cross_hbm, bf16[256,256]{1,0:T(8,128)(2,1)} %constant.20.clone.lag_hbm), custom_call_target="tpu_custom_call" | custom-call | tf_op jit(solution)/shard_map/lags/pallas_call | solution.py:471

commit v5 on v4

--- a/solution.py
+++ b/solution.py
@@ -460,7 +460,7 @@
             vm(blocks, channels, 1536), vm(PAST, blocks * channels), vm(PAST, blocks * channels), vm(128, HALF),
             vm(32, 2, 128, 128), vm(32, 128, 128), vm(32, 2, 128, 128), vm(32, 128, 128), vm(128, 1536),
             vm(32, 16, 512), vm(32, 16, 256), vm(8, 32, 16, 512), vm(8, 32, 16, 256),
-            vm(96 * PITCH, 128, dtype=F32), vm(2, 96 * PITCH, 128, dtype=F32), vm(BINS * PITCH, 128, dtype=F32),
+            vm(97 * PITCH, 128, dtype=F32), vm(2, 97 * PITCH, 128, dtype=F32), vm((BINS + 1) * PITCH, 128, dtype=F32),
             vm(channels, 2, BINS, 128), vm(4, 2, CHUNKS[0][1], 128),
             dma((8,)), dma((9,)), dma((2,)), dma((2, len(CHUNKS))), dma((2, len(CHUNKS))), dma((2,)), dma((2,)), dma((4,)),
             dma((2, 4)), dma((2, 4)), dma((2, 4)), dma((2, 4)), dma, dma, dma((len(CHUNKS),))],

time: 116 us -> 116 us (level)
  no operation moved by 1% of the time
where the time goes in v5:
time: 116 us
  Pallas kernels  115 us (99%)
    pallas_call x1, Pallas kernels, on_device(): pl.pallas_call(whole_kernel, out_shape=jax.ShapeDtypeStruct((channels, 2,...  111 us
    pallas_call x1, Pallas kernels, on_device(): pl.pallas_call(lag_kernel, out_shape=jax.ShapeDtypeStruct((SLOTS, channel...  4.85 us

profile of v5, /device:TPU:1, one launch (start us, length us, event | category | flops | bytes accessed | tf_op | source)
XLA Modules:
  0.0 116.1 jit_solution(17885721859737699063)
XLA Ops:
  0.7 110.5 %cross.1.cross_hbm = bf16[64,2,128,128]{3,2,1,0:T(8,128)(2,1)} custom-call(s32[1]{0:T(128)S(6)} %copy.12.counts, bf16[32,64,1536]{2,1,0:T(8,128)(2,1)} %rec_hbm.1, f32[1,201]{1,0:T(1,128)} %bitcast.4, s32[4,32]{1,0:T(4,128)} %bitcast.3, bf16[512,256]{1,0:T(8,128)(2,1)} %constant.14.clone.fwd_hbm, bf16[256,512]{1,0:T(8,128)(2,1)} %constant.15.clone.fwd_t_hbm, ...), custom_call_target="tpu_custom_call" | custom-call | tf_op jit(solution)/shard_map/cross/pallas_call | solution.py:451
  111.2 4.9 %lags.1 = bf16[4,64,32,256]{3,2,1,0:T(8,128)(2,1)} custom-call(bf16[64,2,128,128]{3,2,1,0:T(8,128)(2,1)} %cross.1.cross_hbm, bf16[256,256]{1,0:T(8,128)(2,1)} %constant.20.clone.lag_hbm), custom_call_target="tpu_custom_call" | custom-call | tf_op jit(solution)/shard_map/lags/pallas_call | solution.py:471

commit v6 on v5

--- a/solution.py
+++ b/solution.py
@@ -259,7 +259,8 @@
         p12[:, :, (w - 1) * 256 : w * 256] = dot(pick[...], v).astype(BF).reshape(wide, 16, 256)
     send_sources(p12, s12, 0)
 
-    lax.fori_loop(FIRST, groups, next12, 0)
+    lax.fori_loop(FIRST, 6, next12, 0)
+    lax.fori_loop(6, groups, group12, 0)
 
     def arrived(landing, ws):
         some = landing.at[0, pl.ds(0, wide - 1)]
@@ -309,6 +310,7 @@
     v = (dot(first, fwd[0:HALF, :]) + dot(second, fwd[HALF:, :])).astype(BF)
     p0[...] = dot(pick[...], v).astype(BF).reshape(wide, 16, 256)
     send_sources(p0, s0, 1)
+    lax.fori_loop(6, groups, send12, 0)
 
     def group0(gi, _):
         g = group_at(gi)

time: 116 us -> 116 us (level)
  no operation moved by 1% of the time
where the time goes in v6:
time: 116 us
  Pallas kernels  115 us (99%)
    pallas_call x1, Pallas kernels, on_device(): pl.pallas_call(whole_kernel, out_shape=jax.ShapeDtypeStruct((channels, 2,...  111 us
    pallas_call x1, Pallas kernels, on_device(): pl.pallas_call(lag_kernel, out_shape=jax.ShapeDtypeStruct((SLOTS, channel...  4.85 us

profile of v6, /device:TPU:1, one launch (start us, length us, event | category | flops | bytes accessed | tf_op | source)
XLA Modules:
  0.0 116.1 jit_solution(7569080316948379910)
XLA Ops:
  0.7 110.5 %cross.1.cross_hbm = bf16[64,2,128,128]{3,2,1,0:T(8,128)(2,1)} custom-call(s32[1]{0:T(128)S(6)} %copy.12.counts, bf16[32,64,1536]{2,1,0:T(8,128)(2,1)} %rec_hbm.1, f32[1,201]{1,0:T(1,128)} %bitcast.4, s32[4,32]{1,0:T(4,128)} %bitcast.3, bf16[512,256]{1,0:T(8,128)(2,1)} %constant.14.clone.fwd_hbm, bf16[256,512]{1,0:T(8,128)(2,1)} %constant.15.clone.fwd_t_hbm, ...), custom_call_target="tpu_custom_call" | custom-call | tf_op jit(solution)/shard_map/cross/pallas_call | solution.py:453
  111.2 4.9 %lags.1 = bf16[4,64,32,256]{3,2,1,0:T(8,128)(2,1)} custom-call(bf16[64,2,128,128]{3,2,1,0:T(8,128)(2,1)} %cross.1.cross_hbm, bf16[256,256]{1,0:T(8,128)(2,1)} %constant.20.clone.lag_hbm), custom_call_target="tpu_custom_call" | custom-call | tf_op jit(solution)/shard_map/lags/pallas_call | solution.py:473
